TPU v7x, 512 devices: a whole 4x8x8 slice. The times are simulated.
512 devices in a mesh: gx: 64 (over y, x, core), ta: 8 (over z).
Axes of the slice: x: 4, y: 8, z: 8, core: 2. Of those that a mesh axis runs over, the one named last changes fastest.
Arguments:
- field: bfloat16 [20, 8, 64, 128, 128], P(None, 'ta', 'gx'), may hold values from -6 to 6
- spectral_weight: float32 [2, 24, 576, 4, 20, 20], P(None, 'ta', 'gx'), may hold values from -6 to 6
- local_weight: float32 [20, 20], replicated, may hold values from -1.25 to 1.25
- cotangent: bfloat16 [20, 8, 64, 128, 128], P(None, 'ta', 'gx'), may hold values from -6 to 6
Outputs:
- layer_out: float32 [20, 8, 64, 128, 128], P(None, 'ta', 'gx')
- grad_field: float32 [20, 8, 64, 128, 128], P(None, 'ta', 'gx')
- grad_spectral: float32 [2, 24, 576, 4, 20, 20], P(None, 'ta', 'gx')
All inputs are finite; a program needn't handle non-finite values.
Results may differ from a plain program's by a relative error of at most 0.0003.
Values sent between devices are 32-bit elements; how exact they have to be, the bound alone decides.
A program may use at most 64 MiB of HBM per device.

v0:
```python
import math

import jax
import jax.numpy as jnp
from jax import lax
from jax.sharding import PartitionSpec as P

MODES = 12
KT = 4
KF = 24


HIGHEST = lax.Precision.HIGHEST


def contract(formula, left, right):
    return jnp.einsum(formula, left, right, precision=HIGHEST)


def kept_frequencies():
    position = jnp.arange(KF, dtype=jnp.int32)
    return jnp.where(position < MODES, position, position - KF)


def phase_tables(period, positions, frequencies):
    phase_turns = positions[:, None] * frequencies[None, :] % period
    angles = phase_turns.astype(jnp.float32) * (2.0 * math.pi / period)
    return (jnp.cos(angles), jnp.sin(angles))


def time_weights():
    return jnp.where(jnp.arange(KT, dtype=jnp.int32) == 0, 1.0, 2.0).astype(jnp.float32)


def time_analysis(block_data, positions, period, factor):
    cos_t, sin_t = phase_tables(period, positions, jnp.arange(KT, dtype=jnp.int32))
    real_in = block_data[:, :, 0]
    imag_in = block_data[:, :, 1]
    real_part = contract("ctkp,tm->ckpm", real_in, cos_t) + contract(
        "ctkp,tm->ckpm", imag_in, sin_t
    )
    imag_part = contract("ctkp,tm->ckpm", imag_in, cos_t) - contract(
        "ctkp,tm->ckpm", real_in, sin_t
    )
    return jnp.stack([real_part, imag_part], 1) * factor


def time_synthesis(block_data, positions, period):
    cos_t, sin_t = phase_tables(period, positions, jnp.arange(KT, dtype=jnp.int32))
    weights = time_weights()
    real_in = block_data[:, 0] * weights
    imag_in = block_data[:, 1] * weights
    real_part = contract("ckpm,tm->ctkp", real_in, cos_t) - contract(
        "ckpm,tm->ctkp", imag_in, sin_t
    )
    imag_part = contract("ckpm,tm->ctkp", real_in, sin_t) + contract(
        "ckpm,tm->ctkp", imag_in, cos_t
    )
    return jnp.stack([real_part, imag_part], 2)


def to_modes(field, factor):
    chans, local_steps, planes, cells_y, cells_z = field.shape
    frequencies = kept_frequencies()
    cos_z, sin_z = phase_tables(cells_z, jnp.arange(cells_z, dtype=jnp.int32), frequencies)
    cos_y, sin_y = phase_tables(cells_y, jnp.arange(cells_y, dtype=jnp.int32), frequencies)
    along_z = contract("ctxyz,zk->ctxyk", field, jnp.concatenate([cos_z, -sin_z], 1))
    real_z = along_z[..., :KF]
    imag_z = along_z[..., KF:]
    real_y = contract("ctxyk,yj->ctxjk", real_z, cos_y) + contract("ctxyk,yj->ctxjk", imag_z, sin_y)
    imag_y = contract("ctxyk,yj->ctxjk", imag_z, cos_y) - contract("ctxyk,yj->ctxjk", real_z, sin_y)
    stacked = jnp.stack([real_y, imag_y], 2).reshape(chans, local_steps, 2, planes, KF * KF)
    block_data = lax.all_to_all(stacked, "gx", split_axis=4, concat_axis=3, tiled=True)
    cells_x = block_data.shape[3]
    cos_x, sin_x = phase_tables(cells_x, jnp.arange(cells_x, dtype=jnp.int32), frequencies)
    real_in = block_data[:, :, 0]
    imag_in = block_data[:, :, 1]
    real_part = contract("ctxp,xi->ctip", real_in, cos_x) + contract(
        "ctxp,xi->ctip", imag_in, sin_x
    )
    imag_part = contract("ctxp,xi->ctip", imag_in, cos_x) - contract(
        "ctxp,xi->ctip", real_in, sin_x
    )
    x_modes = jnp.stack([real_part, imag_part], 2)
    total_steps = local_steps * lax.axis_size("ta")
    positions = lax.axis_index("ta") * local_steps + jnp.arange(local_steps, dtype=jnp.int32)
    partial_sum = time_analysis(x_modes, positions, total_steps, factor)
    return lax.psum_scatter(partial_sum, "ta", scatter_dimension=2, tiled=True)


def from_modes(spectrum, local_steps, planes, cells_y, cells_z, factor):
    frequencies = kept_frequencies()
    total_steps = local_steps * lax.axis_size("ta")
    positions = lax.axis_index("ta") * local_steps + jnp.arange(local_steps, dtype=jnp.int32)
    time_modes = time_synthesis(
        lax.all_gather(spectrum, "ta", axis=2, tiled=True), positions, total_steps
    )
    cells_x = planes * lax.axis_size("gx")
    cos_x, sin_x = phase_tables(cells_x, jnp.arange(cells_x, dtype=jnp.int32), frequencies)
    real_in = time_modes[:, :, 0]
    imag_in = time_modes[:, :, 1]
    real_x = contract("ctkp,xk->ctxp", real_in, cos_x) - contract("ctkp,xk->ctxp", imag_in, sin_x)
    imag_x = contract("ctkp,xk->ctxp", real_in, sin_x) + contract("ctkp,xk->ctxp", imag_in, cos_x)
    stacked = jnp.stack([real_x, imag_x], 2)
    cos_y, sin_y = phase_tables(cells_y, jnp.arange(cells_y, dtype=jnp.int32), frequencies)
    cos_z, sin_z = phase_tables(cells_z, jnp.arange(cells_z, dtype=jnp.int32), frequencies)
    block_data = lax.all_to_all(stacked, "gx", split_axis=3, concat_axis=4, tiled=True)
    chans = block_data.shape[0]
    grid = block_data.reshape(chans, block_data.shape[1], 2, block_data.shape[3], KF, KF)
    real_y = contract("ctxjk,yj->ctxyk", grid[:, :, 0], cos_y) - contract(
        "ctxjk,yj->ctxyk", grid[:, :, 1], sin_y
    )
    imag_y = contract("ctxjk,yj->ctxyk", grid[:, :, 0], sin_y) + contract(
        "ctxjk,yj->ctxyk", grid[:, :, 1], cos_y
    )
    result = contract("ctxyk,zk->ctxyz", real_y, cos_z) - contract("ctxyk,zk->ctxyz", imag_y, sin_z)
    return result * factor


def gelu_parts(pre_act):
    normal_cdf = 0.5 * (1.0 + lax.erf(pre_act * (1.0 / math.sqrt(2.0))))
    density = jnp.exp(-0.5 * pre_act * pre_act) * (1.0 / math.sqrt(2.0 * math.pi))
    return (pre_act * normal_cdf, normal_cdf + pre_act * density)


def shards(field, spectral_weight, local_weight, cotangent):
    field = field.astype(jnp.float32)
    cotangent = cotangent.astype(jnp.float32)
    chans, local_steps, planes, cells_y, cells_z = field.shape
    total_cells = (
        local_steps * lax.axis_size("ta") * planes * lax.axis_size("gx") * cells_y * cells_z
    )
    factor = 1.0 / math.sqrt(total_cells)
    weight_real = spectral_weight[0]
    weight_imag = spectral_weight[1]
    spectrum = to_modes(field, factor)
    spec_real = spectrum[:, 0]
    spec_imag = spectrum[:, 1]
    mixed_real = contract("ckpm,kpmcd->dkpm", spec_real, weight_real) - contract(
        "ckpm,kpmcd->dkpm", spec_imag, weight_imag
    )
    mixed_imag = contract("ckpm,kpmcd->dkpm", spec_real, weight_imag) + contract(
        "ckpm,kpmcd->dkpm", spec_imag, weight_real
    )
    mixed_modes = jnp.stack([mixed_real, mixed_imag], 1)
    pre_act = contract("cd,ctxyz->dtxyz", local_weight, field) + from_modes(
        mixed_modes, local_steps, planes, cells_y, cells_z, factor
    )
    layer_out, derivative = gelu_parts(pre_act)
    upstream = cotangent * derivative
    grad_modes = to_modes(upstream, factor)
    grad_real = grad_modes[:, 0]
    grad_imag = grad_modes[:, 1]
    weights = time_weights()[None, None, :, None, None]
    out_real = contract("ckpm,dkpm->kpmcd", spec_real, grad_real) + contract(
        "ckpm,dkpm->kpmcd", spec_imag, grad_imag
    )
    out_imag = contract("ckpm,dkpm->kpmcd", spec_real, grad_imag) - contract(
        "ckpm,dkpm->kpmcd", spec_imag, grad_real
    )
    grad_spectral = jnp.stack([out_real * weights, out_imag * weights], 0)
    back_real = contract("dkpm,kpmcd->ckpm", grad_real, weight_real) + contract(
        "dkpm,kpmcd->ckpm", grad_imag, weight_imag
    )
    back_imag = contract("dkpm,kpmcd->ckpm", grad_imag, weight_real) - contract(
        "dkpm,kpmcd->ckpm", grad_real, weight_imag
    )
    back_modes = jnp.stack([back_real, back_imag], 1)
    grad_field = contract("cd,dtxyz->ctxyz", local_weight, upstream) + from_modes(
        back_modes, local_steps, planes, cells_y, cells_z, factor
    )
    return (layer_out, grad_field, grad_spectral)


def solution(mesh):
    placed = (
        P(None, "ta", "gx", None, None),
        P(None, "ta", "gx", None, None, None),
        P(),
        P(None, "ta", "gx", None, None),
    )
    return jax.shard_map(
        shards,
        mesh=mesh,
        in_specs=placed,
        out_specs=(
            P(None, "ta", "gx", None, None),
            P(None, "ta", "gx", None, None),
            P(None, "ta", "gx", None, None, None),
        ),
        check_vma=False,
    )
```

profile of v0, /device:TPU:1, one launch (start us, length us, event | category | flops | bytes accessed | tf_op | source)
XLA Modules:
  0.0 421.9 jit_solution(8709068495133324922)
XLA Ops:
  9.1 1.4 fusion.62
  10.5 1.4 fusion.61
  11.9 1.4 fusion.18
  13.5 1.4 fusion.19
  15.5 1.3 reshape.520
  16.8 11.6 %all-to-all-start = ((f32[64,1,360]{2,1,0:T(1,128)}), f32[64,1,360]{2,1,0:T(1,128)S(1)}, u32[]{:S(2)}, u32[]{:S(2)}) async-start(f32[64,1,360]{2,1,0:T(1,128)} %reshape.520), calls=%async_computation | async-start | bytes 196608 | tf_op jit(solution)/shard_map/all_to_all | solution.py:73
  28.7 10.2 %all-to-all-done = f32[64,1,360]{2,1,0:T(1,128)S(1)} async-done(((f32[64,1,360]{2,1,0:T(1,128)}), f32[64,1,360]{2,1,0:T(1,128)S(1)}, u32[]{:S(2)}, u32[]{:S(2)}) %all-to-all-start) | async-done | bytes 92192 | tf_op jit(solution)/shard_map/all_to_all | solution.py:73
  44.9 1.2 maximum_multiply_fusion
  46.2 2.7 slice_bitcast_fusion.1
  48.9 1.5 copy.132
  50.4 2.2 copy.129
  52.6 1.3 dynamic-slice
  54.6 67.1 %all-reduce.5.cloned.1.call-done = f32[20,2,24,9,4]{0,4,3,2,1:T(4,128)} async-done(((f32[20,2,24,9,4]{0,4,3,2,1:T(4,128)}), f32[20,2,24,9,4]{0,4,3,2,1:T(4,128)}) %all-reduce.5.cloned.1.call-update) | async-done | bytes 138256
  122.6 2.2 fusion.356
  124.7 2.2 fusion.354
  126.9 2.2 fusion.357
  129.1 2.2 fusion.355
  131.3 21.4 %all_gather.6 = f32[20,2,24,9,4]{0,4,3,2,1:T(4,128)S(1)} all-gather(f32[20,2,3,9,4]{0,4,3,2,1:T(4,128)S(1)} %pad_maximum_fusion.3), channel_id=1, replica_groups=mesh['gx'=64,'ta'=8] {'ta'}, dimensions={2}, use_global_device_ids=true | all-gather | bytes 155520 | tf_op jit(solution)/shard_map/all_gather | solution.py:96
  153.7 1.6 fusion.35
  155.2 1.6 fusion.37
  156.8 1.6 fusion.33
  163.7 1.4 fusion.24
  165.1 1.3 fusion.25
  167.6 1.7 reshape.522
  169.3 29.7 %all_to_all.42 = f32[64,1,360]{2,1,0:T(1,128)S(1)} all-to-all(f32[64,1,360]{2,1,0:T(1,128)S(1)} %reshape.522), channel_id=1, replica_groups=mesh['gx'=64,'ta'=8] {'gx'}, dimensions={0} | all-to-all | bytes 184320 | tf_op jit(solution)/shard_map/all_to_all | solution.py:107
  199.9 1.3 reshape.523
  201.1 2.6 fusion.352
  204.9 1.8 fusion.158
  206.7 1.7 fusion.175
  211.8 3.2 fusion.53
  215.0 2.2 fusion.55
  217.3 2.5 fusion.10
  220.9 1.6 fusion.13
  222.6 1.6 fusion.64
  224.1 1.4 fusion.63
  225.6 2.1 fusion.16
  227.7 1.7 stack.94
  229.4 3.1 fusion.17
  232.5 1.8 stack.93
  236.2 2.3 reshape.524
  238.6 4.4 %all-to-all-start.2 = ((f32[64,1,360]{2,1,0:T(1,128)}), f32[64,1,360]{2,1,0:T(1,128)S(1)}, u32[]{:S(2)}, u32[]{:S(2)}) async-start(f32[64,1,360]{2,1,0:T(1,128)} %reshape.524), calls=%async_computation.2 | async-start | bytes 196608 | tf_op jit(solution)/shard_map/all_to_all | solution.py:73
  245.1 8.6 %all-to-all-done.2 = f32[64,1,360]{2,1,0:T(1,128)S(1)} async-done(((f32[64,1,360]{2,1,0:T(1,128)}), f32[64,1,360]{2,1,0:T(1,128)S(1)}, u32[]{:S(2)}, u32[]{:S(2)}) %all-to-all-start.2) | async-done | bytes 92192 | tf_op jit(solution)/shard_map/all_to_all | solution.py:73
  254.6 1.3 reshape.525
  255.9 2.6 fusion.351
  259.6 1.4 fusion.73
  262.9 1.6 fusion.22
  265.6 1.2 maximum_multiply_fusion.1
  266.8 1.7 multiply_bitcast_fusion
  268.5 1.3 copy.109
  269.8 66.3 %all-reduce.7.cloned.1.call-done = f32[20,2,24,9,4]{0,4,3,2,1:T(4,128)} async-done(((f32[20,2,24,9,4]{0,4,3,2,1:T(4,128)}), f32[20,2,24,9,4]{0,4,3,2,1:T(4,128)}) %all-reduce.7.cloned.1.call-update) | async-done | bytes 138256
  336.9 1.3 fusion.361
  338.3 1.3 fusion.358
  339.6 1.4 fusion.360
  341.0 1.3 fusion.359
  342.4 21.4 %all_gather.7 = f32[20,2,24,9,4]{0,4,3,2,1:T(4,128)S(1)} all-gather(f32[20,2,3,9,4]{0,4,3,2,1:T(4,128)S(1)} %pad_maximum_fusion.4), channel_id=1, replica_groups=mesh['gx'=64,'ta'=8] {'ta'}, dimensions={2}, use_global_device_ids=true | all-gather | bytes 155520 | tf_op jit(solution)/shard_map/all_gather | solution.py:96
  370.3 1.3 reshape.526
  371.6 19.7 %all-to-all-start.3 = ((f32[64,1,360]{2,1,0:T(1,128)}), f32[64,1,360]{2,1,0:T(1,128)S(1)}, u32[]{:S(2)}, u32[]{:S(2)}) async-start(f32[64,1,360]{2,1,0:T(1,128)} %reshape.526), calls=%async_computation.3 | async-start | bytes 196608 | tf_op jit(solution)/shard_map/all_to_all | solution.py:107
  391.3 1.4 multiply_bitcast_fusion.2
  392.8 1.9 pad_maximum_fusion
  394.7 7.0 %all-to-all-done.3 = f32[64,1,360]{2,1,0:T(1,128)S(1)} async-done(((f32[64,1,360]{2,1,0:T(1,128)}), f32[64,1,360]{2,1,0:T(1,128)S(1)}, u32[]{:S(2)}, u32[]{:S(2)}) %all-to-all-start.3) | async-done | bytes 92192 | tf_op jit(solution)/shard_map/all_to_all | solution.py:107
  405.9 2.2 fusion.49
  408.1 2.2 fusion.51
  410.4 2.9 fusion.7
  413.3 1.3 copy.110
  (140 shorter events, 44.1 us)
Async XLA Ops:
  7.2 1.1 copy-start
  7.2 157.9 %copy-start.12 = (s32[24]{0:T(128)}, s32[24]{0:T(128)S(1)}, u32[]{:S(2)}) copy-start(s32[24]{0:T(128)S(1)} %compare_select_fusion) | copy-start | bytes 292
  7.3 1.7 copy-start.16
  7.3 1.7 copy-start.18
  16.8 22.2 %all-to-all-start = ((f32[64,1,360]{2,1,0:T(1,128)}), f32[64,1,360]{2,1,0:T(1,128)S(1)}, u32[]{:S(2)}, u32[]{:S(2)}) async-start(f32[64,1,360]{2,1,0:T(1,128)} %reshape.520), calls=%async_computation | async-start | bytes 196608 | tf_op jit(solution)/shard_map/all_to_all | solution.py:73
  28.4 93.3 %all-reduce.5.cloned.1.call-start = ((), (), s32[]{:S(2)}) async-start(), calls=%async_computation.4 | async-start | bytes 1769472
  28.7 15.9 %copy-start.24 = (f32[4]{0:T(128)}, f32[4]{0:T(128)S(1)}, u32[]{:S(2)}) copy-start(f32[4]{0:T(128)S(1)} %get-tuple-element.37) | copy-start | bytes 52
  28.7 15.9 %copy-start.26 = (f32[4]{0:T(128)}, f32[4]{0:T(128)S(1)}, u32[]{:S(2)}) copy-start(f32[4]{0:T(128)S(1)} %get-tuple-element.38) | copy-start | bytes 52
  54.6 102.2 %copy-start.22 = (f32[4]{0:T(128)}, f32[4]{0:T(128)S(1)}, u32[]{:S(2)}) copy-start(f32[4]{0:T(128)S(1)} %compare_select_fusion.3) | copy-start | bytes 52
  122.5 4.4 %copy-start.8 = (f32[20,1,3,9,4]{0,4,3,2,1:T(4,128)}, f32[20,1,3,9,4]{0,4,3,2,1:T(4,128)S(1)}, u32[]{:S(2)}) copy-start(f32[20,1,3,9,4]{0,4,3,2,1:T(4,128)S(1)} %get-tuple-element.20) | copy-start | bytes 25924
  122.6 6.5 %copy-start.10 = (f32[20,1,3,9,4]{0,4,3,2,1:T(4,128)}, f32[20,1,3,9,4]{0,4,3,2,1:T(4,128)S(1)}, u32[]{:S(2)}) copy-start(f32[20,1,3,9,4]{0,4,3,2,1:T(4,128)S(1)} %get-tuple-element.19) | copy-start | bytes 25924
  209.6 5.4 %copy-start.7 = (f32[128,480]{0,1:S(1)}, f32[128,480]{0,1}, u32[]{:S(2)}) copy-start(f32[128,480]{0,1} %fusion.175) | copy-start | bytes 737284
  209.6 5.4 %copy-start.13 = (s32[24]{0:T(128)S(1)}, s32[24]{0:T(128)}, u32[]{:S(2)}) copy-start(s32[24]{0:T(128)} %copy-done.12) | copy-start | bytes 292
  215.0 2.3 copy-start.20
  217.3 2.5 copy-start.15
  219.8 1.1 copy-start.1
  219.8 1.1 copy-start.17
  219.8 1.1 copy-start.19
  220.9 4.6 %copy-start.2 = (f32[20,128,128]{2,0,1:T(8,128)}, f32[20,128,128]{2,0,1:T(8,128)S(1)}, u32[]{:S(2)}) copy-start(f32[20,128,128]{2,0,1:T(8,128)S(1)} %fusion.6) | copy-start | bytes 3932164
  222.5 3.0 copy-start.4
  232.5 10.6 %copy-start.11 = (f32[20,1,3,9,4]{0,4,3,2,1:T(4,128)S(1)}, f32[20,1,3,9,4]{0,4,3,2,1:T(4,128)}, u32[]{:S(2)}) copy-start(f32[20,1,3,9,4]{0,4,3,2,1:T(4,128)} %copy-done.10) | copy-start | bytes 25924
  232.5 11.6 %copy-start.9 = (f32[20,1,3,9,4]{0,4,3,2,1:T(4,128)S(1)}, f32[20,1,3,9,4]{0,4,3,2,1:T(4,128)}, u32[]{:S(2)}) copy-start(f32[20,1,3,9,4]{0,4,3,2,1:T(4,128)} %copy-done.8) | copy-start | bytes 25924
  238.6 15.2 %all-to-all-start.2 = ((f32[64,1,360]{2,1,0:T(1,128)}), f32[64,1,360]{2,1,0:T(1,128)S(1)}, u32[]{:S(2)}, u32[]{:S(2)}) async-start(f32[64,1,360]{2,1,0:T(1,128)} %reshape.524), calls=%async_computation.2 | async-start | bytes 196608 | tf_op jit(solution)/shard_map/all_to_all | solution.py:73
  243.0 93.1 %all-reduce.7.cloned.1.call-start = ((), (), s32[]{:S(2)}) async-start(), calls=%async_computation.5 | async-start | bytes 1769472
  245.1 14.5 %copy-start.14 = (s32[24]{0:T(128)S(1)}, s32[24]{0:T(128)}, u32[]{:S(2)}) copy-start(s32[24]{0:T(128)} %copy-done.12) | copy-start | bytes 292
  258.5 6.8 %copy-start.25 = (f32[4]{0:T(128)S(1)}, f32[4]{0:T(128)}, u32[]{:S(2)}) copy-start(f32[4]{0:T(128)} %copy-done.24) | copy-start | bytes 52
  258.5 6.8 %copy-start.27 = (f32[4]{0:T(128)S(1)}, f32[4]{0:T(128)}, u32[]{:S(2)}) copy-start(f32[4]{0:T(128)} %copy-done.26) | copy-start | bytes 52
  341.0 22.8 %copy-start.23 = (f32[4]{0:T(128)S(1)}, f32[4]{0:T(128)}, u32[]{:S(2)}) copy-start(f32[4]{0:T(128)} %copy-done.22) | copy-start | bytes 52
  369.4 21.9 %copy-start.5 = (f32[3,9,4,20]{2,3,1,0:T(8,128)S(1)}, f32[3,9,4,20]{2,3,1,0:T(8,128)}, u32[]{:S(2)}) copy-start(f32[3,9,4,20]{2,3,1,0:T(8,128)} %copy.108) | copy-start | bytes 25924
  369.4 21.9 %copy-start.6 = (f32[3,9,4,20]{2,3,1,0:T(8,128)S(1)}, f32[3,9,4,20]{2,3,1,0:T(8,128)}, u32[]{:S(2)}) copy-start(f32[3,9,4,20]{2,3,1,0:T(8,128)} %copy.107) | copy-start | bytes 25924
  371.6 30.2 %all-to-all-start.3 = ((f32[64,1,360]{2,1,0:T(1,128)}), f32[64,1,360]{2,1,0:T(1,128)S(1)}, u32[]{:S(2)}, u32[]{:S(2)}) async-start(f32[64,1,360]{2,1,0:T(1,128)} %reshape.526), calls=%async_computation.3 | async-start | bytes 196608 | tf_op jit(solution)/shard_map/all_to_all | solution.py:107
  408.1 2.3 copy-start.3
  408.1 2.3 copy-start.21
Sparse Core Ops, SparseCore 0:
  46.3 75.3 all-reduce.4
  267.0 69.0 all-reduce.6
where the time goes:
time: 427 us; the launch traced here: 422 us
  waiting for transfers between devices  159 us (37%)
  matrix products  76.4 us (18%)
  blocking collectives  72.5 us (17%)
  local copies, waits for them, and re-layouts  48 us (11%)
  starting transfers between devices  36.1 us (8%)
  between operations  16 us (4%)
  other arithmetic  13.6 us (3%)
    unnamed x4, waiting for transfers between devices  133 us
    dot_general x48, matrix products, contract(): return jnp.einsum(formula, left, right, precision=HIGHEST)  68.8 us
    all_gather x2, blocking collectives, from_modes(): lax.all_gather(spectrum, 'ta', axis=2, tiled=True)  42.8 us
    all_to_all x1, blocking collectives, from_modes(): lax.all_to_all(stacked, 'gx', split_axis=3, concat_axis=4, tiled=True)  29.7 us
    unnamed x75, local copies, waits for them, and re-layouts  20.5 us
    all_to_all x1, starting transfers between devices, from_modes(): lax.all_to_all(stacked, 'gx', split_axis=3, concat_axis=4, tiled=True)  19.7 us
    all_to_all x2, waiting for transfers between devices, to_modes(): lax.all_to_all(stacked, 'gx', split_axis=4, concat_axis=3, tiled=True)  18.8 us
    all_to_all x2, starting transfers between devices, to_modes(): lax.all_to_all(stacked, 'gx', split_axis=4, concat_axis=3, tiled=True)  16.1 us
  transfers between devices with their start and end apart: 5, of which 5 were waited for; matrix products, arithmetic and copies ran while one was open for 4% of the time, Pallas kernels for 0%

commit v1 on v0

v1 whole, which is shorter than its diff:
```python
import functools
import math

import jax
import jax.numpy as jnp
import ml_dtypes
import numpy as np
from jax import lax
from jax.experimental import pallas as pl
from jax.experimental.pallas import tpu as pltpu
from jax.sharding import PartitionSpec as P

KT = 4
STRIDE = 32
LANES = 128
F32 = jnp.float32
BF16 = jnp.bfloat16


class Sizes:
    def __init__(self, gx, ta, chans, kf, cells):
        self.gx, self.ta, self.chans, self.kf, self.cells = gx, ta, chans, kf, cells
        self.nxc = 8 if gx % 8 == 0 else 2
        self.ny = gx // self.nxc
        self.pb = kf * kf // gx
        self.ib = kf // ta
        self.width = 2 * chans
        self.per = LANES // self.width
        self.tiles = -(-self.pb // self.per)
        self.rows = 8 * ta
        self.modes = self.ib * self.pb * KT
        self.fper = LANES // STRIDE
        self.ftiles = -(-kf // self.fper)


def split(table):
    table = table.astype(np.float32)
    high = table.astype(ml_dtypes.bfloat16)
    low = (table - high.astype(np.float32)).astype(ml_dtypes.bfloat16)
    return high, low


def two_terms(table):
    high, low = split(table)
    return np.concatenate(
        [np.concatenate([high, high], 1), np.concatenate([low, np.zeros_like(low)], 1)], 0
    )


def make_tables(n):
    half = n.kf // 2
    freq = np.where(np.arange(n.kf) < half, np.arange(n.kf), np.arange(n.kf) - n.kf)
    angle = 2 * np.pi * ((np.arange(n.cells)[:, None] * freq[None, :]) % n.cells) / n.cells
    cos, sin = np.cos(angle), np.sin(angle)
    grid_in = two_terms(np.concatenate([cos.T, sin.T], 0))
    along_z = np.concatenate(
        [np.concatenate([cos.T, sin.T], 1), np.concatenate([-sin.T, cos.T], 1)], 0
    )
    high, low = split(along_z)
    z_out = np.zeros((2 * LANES, 2 * n.cells), ml_dtypes.bfloat16)
    z_out[: 2 * n.kf] = high
    z_out[2 * n.kf : 4 * n.kf] = high
    z_out[LANES : LANES + 2 * n.kf] = low
    high, low = split(np.concatenate([cos, -sin], 1))
    y_out = np.concatenate([high, high, low], 1)
    cells_x = n.gx
    place = np.arange(cells_x)
    sent_by = (place % n.ny) * n.nxc + place // n.ny
    freq_rows = np.zeros((n.rows,), np.int64)
    used = np.zeros((n.rows,), np.float64)
    for block in range(n.ta):
        for i in range(n.ib):
            freq_rows[8 * block + i] = freq[block * n.ib + i]
            used[8 * block + i] = 1.0
    angle = 2 * np.pi * ((freq_rows[:, None] * sent_by[None, :]) % cells_x) / cells_x
    x_in = two_terms(
        np.concatenate([np.cos(angle), -np.sin(angle)], 1) * used[:, None]
    )
    angle = 2 * np.pi * ((place[:, None] * freq_rows[None, :]) % cells_x) / cells_x
    x_out = two_terms(
        np.concatenate([np.cos(angle) * used, np.sin(angle) * used], 1)
    )
    return grid_in, z_out, y_out, x_in, x_out


def halves(value):
    high = value.astype(BF16).astype(F32)
    return high, value - high


def dot(left, right):
    return jnp.dot(left, right, preferred_element_type=F32)


def roll(value, amount):
    amount = amount % LANES
    return value if amount == 0 else pltpu.roll(value, amount, 1)


def times_i(value, chans):
    lane = lax.broadcasted_iota(jnp.int32, value.shape, 1)
    return jnp.where(lane % (2 * chans) < chans, -roll(value, -chans), roll(value, chans))


def kernel(
    n,
    factor,
    field,
    cotangent,
    weight,
    local,
    grid_in,
    z_out,
    y_out,
    x_in,
    x_out,
    layer_out,
    grad_field,
    spec_out,
    grad_out,
    mixed_local,
    upstream,
    y_cos,
    y_sin,
    z_real,
    z_imag,
    pairs,
    stacked,
    turned,
    sent,
    got,
    send_sem,
    recv_sem,
):
    chans, kf, cells = n.chans, n.kf, n.cells
    gx, ta = lax.axis_index("gx"), lax.axis_index("ta")
    my_y, my_xc = gx // n.nxc, gx % n.nxc
    mesh_ids = pl.DeviceIdType.MESH

    def y_peer(k):
        peer = lax.rem(my_y + k, n.ny)
        return peer, {"gx": peer * n.nxc + my_xc, "ta": ta}

    def xc_peer(k):
        peer = lax.rem(my_xc + k, n.nxc)
        return peer, {"gx": my_y * n.nxc + peer, "ta": ta}

    def t_peer(k):
        peer = lax.rem(ta + k, n.ta)
        return peer, {"gx": gx, "ta": peer}

    along = {
        "y": (n.ny, my_y, y_peer, n.nxc),
        "xc": (n.nxc, my_xc, xc_peer, n.ny),
        "t": (n.ta, ta, t_peer, 8),
    }

    barrier = pltpu.get_barrier_semaphore()
    others = 0
    for axis in ("y", "xc", "t"):
        count, _, peer_of, _ = along[axis]
        for k in range(1, count):
            _, device = peer_of(k)
            pl.semaphore_signal(barrier, inc=1, device_id=device, device_id_type=mesh_ids)
            others += 1

    def all_blocks(index, count, rows):
        block = got.at[index, :, pl.ds(0, (count - 1) * rows), :]
        return pltpu.make_async_remote_copy(
            src_ref=block,
            dst_ref=block,
            send_sem=send_sem.at[index],
            recv_sem=recv_sem.at[index],
            device_id={"gx": gx, "ta": ta},
            device_id_type=mesh_ids,
        )

    def exchange(index, axis):
        count, me, peer_of, rows = along[axis]
        mine = pl.ds(pl.multiple_of(me * rows, rows), rows)
        for k in range(1, count):
            peer, device = peer_of(k)
            pltpu.make_async_remote_copy(
                src_ref=sent.at[index, :, pl.ds(pl.multiple_of(peer * rows, rows), rows), :],
                dst_ref=got.at[index, :, mine, :],
                send_sem=send_sem.at[index],
                recv_sem=recv_sem.at[index],
                device_id=device,
                device_id_type=mesh_ids,
            ).start()
        for q in range(n.tiles):
            got[index, q, mine, :] = sent[index, q, mine, :]

    def arrived(index, axis):
        count, _, _, rows = along[axis]
        all_blocks(index, count, rows).wait_recv()

    def regroup(index):
        for q in range(n.tiles):
            for xc in range(n.nxc):
                sent[index + 1, q, xc * n.ny : (xc + 1) * n.ny, :] = got[
                    index, q, pl.ds(xc, n.ny, stride=n.nxc), :
                ]

    def mix_local(source, transposed, start, stop):
        def step(at, carry):
            rows = pl.ds(pl.multiple_of(at * 16, 16), 16)
            values = [source[c, rows, :].astype(F32) for c in range(chans)]
            for d in range(chans):
                total = None
                for c in range(chans):
                    scale = local[d, c] if transposed else local[c, d]
                    term = values[c] * scale
                    total = term if total is None else total + term
                mixed_local[d, rows, :] = total
            return carry

        lax.fori_loop(start, stop, step, 0)

    def pack(index):
        parts = []
        for source in (y_cos, y_sin):
            high, low = halves(source[...])
            both = jnp.concatenate([high.astype(BF16), low.astype(BF16)], 1)
            out = lax.dot_general(
                grid_in[...], both, (((1,), (1,)), ((), ())), preferred_element_type=F32
            )
            parts.append(out[: 2 * kf] + out[2 * kf :])
        of_cos, of_sin = parts
        real = of_cos[:kf] - of_sin[kf:]
        imag = -(of_sin[:kf] + of_cos[kf:])
        lane = lax.broadcasted_iota(jnp.int32, (kf, LANES), 1)
        for j in range(kf):
            tile = slice((j // n.fper) * LANES, (j // n.fper + 1) * LANES)
            back = (j % n.fper) * STRIDE
            value = jnp.where(
                lane < chans,
                roll(real[:, tile], -back),
                jnp.where(lane < 2 * chans, roll(imag[:, tile], chans - back), 0.0),
            )
            pairs[j * kf : (j + 1) * kf, :] = value
        for q in range(n.tiles):
            total = None
            for r in range(n.per):
                value = roll(pairs[pl.ds(q * n.per + r, n.gx, stride=n.pb), :], r * n.width)
                total = value if total is None else total + value
            sent[index, q, : n.gx, :] = total

    def unpack(index):
        for q in range(n.tiles):
            for r in range(n.per):
                value = roll(got[index, q, : n.gx, :], -r * n.width)
                for xc in range(n.nxc):
                    pairs[
                        pl.ds(n.pb * xc + q * n.per + r, n.ny, stride=n.pb * n.nxc), :
                    ] = value[xc * n.ny : (xc + 1) * n.ny]
        lane = lax.broadcasted_iota(jnp.int32, (kf, LANES), 1)
        for tile in range(n.ftiles):
            real = jnp.zeros((kf, LANES), F32)
            imag = jnp.zeros((kf, LANES), F32)
            for part in range(n.fper):
                j = tile * n.fper + part
                if j >= kf:
                    continue
                value = pairs[j * kf : (j + 1) * kf, :]
                begin = part * STRIDE
                here = (lane >= begin) & (lane < begin + chans)
                real = jnp.where(here, roll(value, begin), real)
                imag = jnp.where(here, roll(value, begin - chans), imag)
            high, low = halves(jnp.concatenate([real, imag], 0))
            pad = jnp.zeros((LANES - 4 * kf, LANES), F32)
            rows = jnp.concatenate([high, low, pad], 0).T.astype(BF16)
            out = dot(jnp.concatenate([rows, rows], 1), z_out[...])
            z_real[tile * LANES : (tile + 1) * LANES, :] = out[:, :cells]
            z_imag[tile * LANES : (tile + 1) * LANES, :] = out[:, cells:]

    def plane(d):
        rows = pl.ds(d, kf, stride=STRIDE)
        high, low = halves(jnp.concatenate([z_real[rows, :], z_imag[rows, :]], 0))
        return dot(y_out[...], jnp.concatenate([high, low, high], 0).astype(BF16))

    def put_y(d, out):
        rows = pl.ds(d, kf, stride=STRIDE)
        y_cos[rows, :] = out[:kf] + out[2 * kf : 3 * kf]
        y_sin[rows, :] = out[kf : 2 * kf] + out[3 * kf :]

    def along_x(table, source, target, rows):
        for q in range(n.tiles):
            value = got[source, q, :rows, :]
            high, low = halves(jnp.concatenate([value, times_i(value, chans)], 0))
            out = dot(table[...], jnp.concatenate([high, low], 0).astype(BF16))
            half = out.shape[0] // 2
            sent[target, q, :half, :] = out[:half] + out[half:]

    def time_in(index, target):
        for q in range(n.tiles):
            steps = [got[index, q, 8 * t : 8 * t + 8, :] for t in range(n.ta)]
            for m in range(KT):
                real = imag = None
                for t in range(n.ta):
                    angle = 2 * math.pi * ((m * t) % n.ta) / n.ta
                    first = steps[t] * (math.cos(angle) * factor)
                    second = steps[t] * (math.sin(angle) * factor)
                    real = first if real is None else real + first
                    imag = second if imag is None else imag + second
                value = real - times_i(imag, chans)
                for r in range(n.per):
                    stacked[
                        pl.ds((q * n.per + r) * KT + m, n.ib, stride=n.pb * KT), :
                    ] = roll(value, -r * n.width)[: n.ib]
        target[...] = stacked[...].T[: n.width]

    def time_out(index):
        stacked[...] = turned[...].T
        weights = [1.0 if m == 0 else 2.0 for m in range(KT)]
        for q in range(n.tiles):
            values = []
            for m in range(KT):
                total = None
                for r in range(n.per):
                    rows = pl.ds((q * n.per + r) * KT + m, n.ib, stride=n.pb * KT)
                    value = roll(stacked[rows, :], r * n.width)
                    total = value if total is None else total + value
                values.append((total, times_i(total, chans)))
            for t in range(n.ta):
                total = None
                for m in range(KT):
                    angle = 2 * math.pi * ((m * t) % n.ta) / n.ta
                    value = values[m][0] * (math.cos(angle) * factor * weights[m])
                    value += values[m][1] * (math.sin(angle) * factor * weights[m])
                    total = value if total is None else total + value
                sent[index, q, 8 * t : 8 * t + n.ib, :] = total

    def analyse_field(c, carry):
        put_y(c, dot(grid_in[:, :cells], field[c]))
        return carry

    lax.fori_loop(0, chans, analyse_field, 0)
    pack(0)
    stacked[...] = jnp.zeros_like(stacked)
    turned[...] = jnp.zeros_like(turned)
    for index in (3, 9):
        sent[index] = jnp.zeros_like(sent[index])
    pl.semaphore_wait(barrier, others)

    def to_owner(index, result, hidden):
        exchange(index, "y")
        hidden(0)
        arrived(index, "y")
        regroup(index)
        exchange(index + 1, "xc")
        hidden(1)
        arrived(index + 1, "xc")
        along_x(x_in, index + 1, index + 2, n.gx)
        exchange(index + 2, "t")
        hidden(2)
        arrived(index + 2, "t")
        time_in(index + 2, result)

    def to_planes(index, hidden):
        time_out(index)
        exchange(index, "t")
        hidden(3)
        arrived(index, "t")
        along_x(x_out, index, index + 1, n.rows)
        exchange(index + 1, "y")
        hidden(4)
        arrived(index + 1, "y")
        regroup(index + 1)
        exchange(index + 2, "xc")
        hidden(5)
        arrived(index + 2, "xc")
        unpack(index + 2)

    chunks = cells // 16
    cuts = [0, chunks // 4, chunks // 2, chunks // 2, chunks // 2, 3 * chunks // 4, chunks]

    def hidden_field(part):
        if cuts[part + 1] > cuts[part]:
            mix_local(field, False, cuts[part], cuts[part + 1])

    def hidden_upstream(part):
        if cuts[part + 1] > cuts[part]:
            mix_local(upstream, True, cuts[part], cuts[part + 1])

    to_owner(0, spec_out, hidden_field)
    real = jnp.zeros((chans, LANES), F32)
    imag = jnp.zeros((chans, LANES), F32)
    for c in range(chans):
        spec_r, spec_i = spec_out[c : c + 1, :], spec_out[chans + c : chans + c + 1, :]
        real += spec_r * weight[0, c] - spec_i * weight[1, c]
        imag += spec_r * weight[1, c] + spec_i * weight[0, c]
    turned[:chans, :] = real
    turned[chans : 2 * chans, :] = imag
    to_planes(3, hidden_field)

    def activate(d, carry):
        pre_act = mixed_local[d] + plane(d)
        normal_cdf = 0.5 * (1.0 + lax.erf(pre_act * (1.0 / math.sqrt(2.0))))
        density = jnp.exp(-0.5 * pre_act * pre_act) * (1.0 / math.sqrt(2.0 * math.pi))
        layer_out[d] = pre_act * normal_cdf
        value = cotangent[d].astype(F32) * (normal_cdf + pre_act * density)
        upstream[d] = value
        high, low = halves(value)
        both = jnp.concatenate([high, low], 0).astype(BF16)
        put_y(d, dot(grid_in[...], both))
        return carry

    lax.fori_loop(0, chans, activate, 0)
    pack(6)
    to_owner(6, grad_out, hidden_upstream)
    grad_r, grad_i = grad_out[:chans, :], grad_out[chans : 2 * chans, :]
    for c in range(chans):
        turned[c : c + 1, :] = jnp.sum(
            weight[0, c] * grad_r + weight[1, c] * grad_i, 0, keepdims=True
        )
        turned[chans + c : chans + c + 1, :] = jnp.sum(
            weight[0, c] * grad_i - weight[1, c] * grad_r, 0, keepdims=True
        )
    to_planes(9, hidden_upstream)

    def finish(c, carry):
        grad_field[c] = mixed_local[c] + plane(c)
        return carry

    lax.fori_loop(0, chans, finish, 0)
    for index, axis in enumerate(("y", "xc", "t", "t", "y", "xc") * 2):
        count, _, _, rows = along[axis]
        all_blocks(index, count, rows).wait_send()


def shards(n, factor, field, spectral_weight, local_weight, cotangent):
    chans, cells = n.chans, n.cells
    tables = [jnp.asarray(table) for table in make_tables(n)]
    weight = spectral_weight.reshape(2, n.modes, chans, chans)
    weight = jnp.transpose(weight, (0, 2, 3, 1))
    weight = jnp.pad(weight, ((0, 0), (0, 0), (0, 0), (0, LANES - n.modes)))
    whole = pl.BlockSpec(memory_space=pltpu.VMEM)
    wide = jax.ShapeDtypeStruct((chans, cells, cells), F32)
    small = jax.ShapeDtypeStruct((n.width, LANES), F32)
    layer_out, grad_field, spec, grad = pl.pallas_call(
        functools.partial(kernel, n, factor),
        out_shape=(wide, wide, small, small),
        in_specs=[whole] * 3 + [pl.BlockSpec(memory_space=pltpu.SMEM)] + [whole] * 5,
        out_specs=(whole,) * 4,
        scratch_shapes=[
            pltpu.VMEM((chans, cells, cells), F32),
            pltpu.VMEM((chans, cells, cells), F32),
            pltpu.VMEM((n.ftiles * LANES, cells), F32),
            pltpu.VMEM((n.ftiles * LANES, cells), F32),
            pltpu.VMEM((n.ftiles * LANES, cells), F32),
            pltpu.VMEM((n.ftiles * LANES, cells), F32),
            pltpu.VMEM((n.kf * n.kf, LANES), F32),
            pltpu.VMEM((LANES, LANES), F32),
            pltpu.VMEM((LANES, LANES), F32),
            pltpu.VMEM((12, n.tiles, max(n.gx, n.rows), LANES), F32),
            pltpu.VMEM((12, n.tiles, max(n.gx, n.rows), LANES), F32),
            pltpu.SemaphoreType.DMA((12,)),
            pltpu.SemaphoreType.DMA((12,)),
        ],
        compiler_params=pltpu.CompilerParams(
            collective_id=0, has_side_effects=True, vmem_limit_bytes=48 * 1024 * 1024
        ),
    )(
        field.reshape(chans, cells, cells),
        cotangent.reshape(chans, cells, cells),
        weight,
        local_weight,
        *tables,
    )
    pairs_shape = (n.ib, n.pb, KT, chans)
    spec_r = spec[:chans, : n.modes].T.reshape(pairs_shape)[..., :, None]
    spec_i = spec[chans:, : n.modes].T.reshape(pairs_shape)[..., :, None]
    grad_r = grad[:chans, : n.modes].T.reshape(pairs_shape)[..., None, :]
    grad_i = grad[chans:, : n.modes].T.reshape(pairs_shape)[..., None, :]
    weights = jnp.where(jnp.arange(KT) == 0, 1.0, 2.0).astype(F32)[None, None, :, None, None]
    spec_r, spec_i = spec_r * weights, spec_i * weights
    grad_spectral = jnp.stack(
        [spec_r * grad_r + spec_i * grad_i, spec_r * grad_i - spec_i * grad_r], 0
    )
    return (layer_out.reshape(field.shape), grad_field.reshape(field.shape), grad_spectral)


def solution(mesh, chans=20, kf=24, cells=128):
    n = Sizes(mesh.shape["gx"], mesh.shape["ta"], chans, kf, cells)
    factor = 1.0 / math.sqrt(n.gx * n.ta * cells * cells)
    grid = P(None, "ta", "gx", None, None)
    modes = P(None, "ta", "gx", None, None, None)
    return jax.shard_map(
        functools.partial(shards, n, factor),
        mesh=mesh,
        in_specs=(grid, modes, P(), grid),
        out_specs=(grid, grid, modes),
        check_vma=False,
    )
```

time: 427 us -> 104 us (0.24); the launches traced: 422 us -> 104 us
  waiting for transfers between devices: 159 us -> 0 us
  Pallas kernels: 0 us -> 88.3 us
  matrix products: 76.4 us -> 0 us
  blocking collectives: 72.5 us -> 0 us
  local copies, waits for them, and re-layouts: 48 us -> 11 us
  starting transfers between devices: 36.1 us -> 0 us
  between operations: 16 us -> 0.78 us
  other arithmetic: 13.6 us -> 3.41 us
    unnamed x4 -> x0, waiting for transfers between devices: 133 us -> none
    pallas_call x0 -> x1, Pallas kernels: none -> 88.3 us  [shards(): pl.pallas_call(functools.partial(kernel, n, factor), out_shape=(wide, wid...]
    dot_general x48 -> x0, matrix products: 68.8 us -> none  [contract(): return jnp.einsum(formula, left, right, precision=HIGHEST)]
    all_gather x2 -> x0, blocking collectives: 42.8 us -> none  [from_modes(): lax.all_gather(spectrum, 'ta', axis=2, tiled=True)]
    all_to_all x3 -> x0, starting transfers between devices: 35.8 us -> none  [the longest x1 19.7 us: from_modes(): lax.all_to_all(stacked, 'gx', split_axis=3, concat_axis=4, tiled=True)]
    all_to_all x1 -> x0, blocking collectives: 29.7 us -> none  [from_modes(): lax.all_to_all(stacked, 'gx', split_axis=3, concat_axis=4, tiled=True)]
    all_to_all x3 -> x0, waiting for transfers between devices: 25.9 us -> none  [the longest x2 18.8 us: to_modes(): lax.all_to_all(stacked, 'gx', split_axis=4, concat_axis=3, tiled=True)]
    unnamed x75 -> x19, local copies, waits for them, and re-layouts: 20.5 us -> 6.61 us
  transfers between devices with their start and end apart: 5 -> 0, of which waited for: 5 -> 0; matrix products, arithmetic and copies ran while one was open for 4% -> 0% of each run, Pallas kernels for 0% -> 0%
where the time goes in v1:
time: 104 us
  Pallas kernels  88.3 us (85%)
  local copies, waits for them, and re-layouts  11 us (11%)
  other arithmetic  3.41 us (3%)
    pallas_call x1, Pallas kernels, shards(): pl.pallas_call(functools.partial(kernel, n, factor), out_shape=(wide, wid...  88.3 us
    unnamed x19, local copies, waits for them, and re-layouts  6.61 us
    reshape x1, local copies, waits for them, and re-layouts, shards(): weight = spectral_weight.reshape(2, n.modes, chans, chans)  2.17 us

profile of v1, /device:TPU:1, one launch (start us, length us, event | category | flops | bytes accessed | tf_op | source)
XLA Modules:
  0.0 103.6 jit_solution(10365661097878291864)
XLA Ops:
  0.6 2.8 %copy.19 = f32[2,3,9,4,20,20]{5,0,4,3,2,1:T(2,128)S(1)} copy(f32[2,3,9,4,20,20]{5,3,4,2,1,0:T(4,128)} %param.10) | data formatting | bytes 691200 | tf_op args[1]
  3.4 0.0 copy-start.1
  3.4 0.0 copy-start.2
  3.5 0.0 copy-start.3
  3.5 0.0 copy-start.4
  3.5 0.0 copy-start.7
  3.5 2.2 %copy.20 = f32[2,108,20,20]{1,3,2,0:T(8,128)} copy(f32[2,108,20,20]{3,0,2,1:T(2,128)S(1)} %bitcast.22) | data formatting | bytes 691200 | tf_op jit(solution)/shard_map/reshape | solution.py:435
  5.7 0.0 copy-start
  5.7 1.1 %pad.4.weight = f32[2,20,20,128]{3,2,1,0:T(8,128)S(1)} pad(f32[2,20,20,108]{3,2,1,0:T(8,128)} %bitcast.23, f32[]{:T(128)} %constant.6.clone.1), padding=0_0x0_0x0_0x0_20 | pad | bytes 755204 | tf_op jit(solution)/shard_map/jit(_pad)/pad | solution.py:437
  6.8 0.0 copy-done.1
  6.8 0.0 copy-done.2
  6.8 0.0 copy-done.3
  6.8 0.0 copy-done.4
  6.8 0.0 copy-done.7
  6.9 0.0 copy-done
  6.9 0.0 copy-start.5
  6.9 0.8 copy-done.5
  7.7 0.0 copy-start.6
  7.7 0.8 copy-done.6
  8.5 88.3 %shard_map.112 = (f32[20,128,128]{2,1,0:T(8,128)S(1)}, f32[20,128,128]{2,1,0:T(8,128)S(1)}, f32[40,128]{1,0:T(8,128)S(1)}, f32[40,128]{1,0:T(8,128)S(1)}) custom-call(bf16[20,128,128]{2,1,0:T(8,128)(2,1)S(1)} %bitcast.20, bf16[20,128,128]{2,1,0:T(8,128)(2,1)S(1)} %bitcast.21, f32[2,20,20,128]{3,2,1,0:T(8,128)S(1)} %pad.4.weight, f32[20,20]{1,0:T(8,128)S(1)} %copy-done.7, ...), custom_call_target="tpu_custom_call" | custom-call | tf_op jit(solution)/shard_map/pallas_call | solution.py:441
  96.9 0.1 copy.23
  97.0 0.1 copy.26
  97.2 0.1 copy.24
  97.3 0.1 copy.21
  97.5 0.1 broadcast_multiply_fusion.1
  97.6 0.3 copy.22
  97.8 0.3 copy.25
  98.1 1.4 %multiply_add_fusion = (f32[1,3,9,4,20,20]{5,3,4,2,1,0:T(4,128)S(1)}, f32[1,3,9,4,20,20]{5,3,4,2,1,0:T(4,128)S(1)}) fusion(f32[3,9,4,20]{3,2,1,0:T(4,128)S(1)} %mul.110, f32[3,9,4,20]{2,3,1,0:T(8,128)S(1)} %copy.25, f32[3,9,4,20]{3,2,1,0:T(4,128)S(1)} %mul.105, f32[3,9,4,20]{2,3,1,0:T(8,128)S(1)} %copy.22), kind=kLoop, calls=%fused_computation.2 | loop fusion | flops 259200 | bytes 380160 | tf_op jit(solution)/shard_map/add | solution.py:479
  99.5 1.9 %pad_maximum_fusion = f32[2,3,9,4,20,20]{5,3,4,2,1,0:T(4,128)} fusion(f32[1,3,9,4,20,20]{5,3,4,2,1,0:T(4,128)S(1)} %get-tuple-element.18, f32[1,3,9,4,20,20]{5,3,4,2,1,0:T(4,128)S(1)} %get-tuple-element.17), kind=kLoop, calls=%fused_computation | loop fusion | flops 86400 | bytes 691200 | tf_op jit(solution)/shard_map/stack | solution.py:478
  101.5 1.1 %copy.31 = f32[20,1,1,128,128]{4,3,2,1,0:T(8,128)} copy(f32[20,1,1,128,128]{4,3,2,1,0:T(8,128)S(1)} %bitcast.19) | data formatting | bytes 2621440
  102.5 1.1 %copy.32 = f32[20,1,1,128,128]{4,3,2,1,0:T(8,128)} copy(f32[20,1,1,128,128]{4,3,2,1,0:T(8,128)S(1)} %bitcast.18) | data formatting | bytes 2621440
  (6 shorter events, 0.1 us)
Async XLA Ops:
  3.4 3.4 %copy-start.1 = (bf16[20,1,1,128,128]{4,3,2,1,0:T(8,128)(2,1)S(1)}, bf16[20,1,1,128,128]{4,3,2,1,0:T(8,128)(2,1)}, u32[]{:S(2)}) copy-start(bf16[20,1,1,128,128]{4,3,2,1,0:T(8,128)(2,1)} %param.12) | copy-start | bytes 1966084
  3.4 3.4 %copy-start.2 = (bf16[256,256]{1,0:T(8,128)(2,1)S(1)}, bf16[256,256]{1,0:T(8,128)(2,1)}, u32[]{:S(2)}) copy-start(bf16[256,256]{1,0:T(8,128)(2,1)} %constant.20.clone.z_out) | copy-start | bytes 393220
  3.5 3.4 %copy-start.3 = (bf16[128,256]{1,0:T(8,128)(2,1)S(1)}, bf16[128,256]{1,0:T(8,128)(2,1)}, u32[]{:S(2)}) copy-start(bf16[128,256]{1,0:T(8,128)(2,1)} %constant.23.clone.x_out) | copy-start | bytes 196612
  3.5 3.4 %copy-start.4 = (bf16[128,256]{1,0:T(8,128)(2,1)S(1)}, bf16[128,256]{1,0:T(8,128)(2,1)}, u32[]{:S(2)}) copy-start(bf16[128,256]{1,0:T(8,128)(2,1)} %constant.22.clone.x_in) | copy-start | bytes 196612
  3.5 3.4 %copy-start.7 = (f32[20,20]{1,0:T(8,128)S(1)}, f32[20,20]{1,0:T(8,128)}, u32[]{:S(2)}) copy-start(f32[20,20]{1,0:T(8,128)} %local.1) | copy-start | bytes 4804
  5.7 1.2 %copy-start = (bf16[20,1,1,128,128]{4,3,2,1,0:T(8,128)(2,1)S(1)}, bf16[20,1,1,128,128]{4,3,2,1,0:T(8,128)(2,1)}, u32[]{:S(2)}) copy-start(bf16[20,1,1,128,128]{4,3,2,1,0:T(8,128)(2,1)} %param.9) | copy-start | bytes 1966084
  6.9 0.8 copy-start.5
  7.7 0.8 copy-start.6

commit v2 on v1

v2 whole, which is shorter than its diff:
```python
import functools
import math

import jax
import jax.numpy as jnp
import ml_dtypes
import numpy as np
from jax import lax
from jax.experimental import pallas as pl
from jax.experimental.pallas import tpu as pltpu
from jax.sharding import PartitionSpec as P

KT = 4
STRIDE = 32
LANES = 128
F32 = jnp.float32
BF16 = jnp.bfloat16


class Sizes:
    def __init__(self, gx, ta, chans, kf, cells):
        self.gx, self.ta, self.chans, self.kf, self.cells = gx, ta, chans, kf, cells
        self.nx = 4 if gx % 8 == 0 else 1
        self.ny = gx // (2 * self.nx)
        self.pb = kf * kf // gx
        self.ib = kf // ta
        self.width = 2 * chans
        self.per = LANES // self.width
        self.tiles = -(-self.pb // self.per)
        self.rows = 4 * ta
        self.blocks = self.ib * self.pb
        self.modes = self.blocks * KT
        self.fper = LANES // STRIDE
        self.ftiles = -(-kf // self.fper)
        self.frows = self.ftiles * LANES


def split(table):
    table = table.astype(np.float32)
    high = table.astype(ml_dtypes.bfloat16)
    low = (table - high.astype(np.float32)).astype(ml_dtypes.bfloat16)
    return high, low


def two_terms(table):
    high, low = split(table)
    return np.concatenate(
        [np.concatenate([high, high], 1), np.concatenate([low, np.zeros_like(low)], 1)], 0
    )


def make_tables(n):
    half = n.kf // 2
    freq = np.where(np.arange(n.kf) < half, np.arange(n.kf), np.arange(n.kf) - n.kf)
    angle = 2 * np.pi * ((np.arange(n.cells)[:, None] * freq[None, :]) % n.cells) / n.cells
    cos, sin = np.cos(angle), np.sin(angle)
    grid_in = two_terms(np.concatenate([cos.T, sin.T], 0))
    along_z = np.concatenate(
        [np.concatenate([cos.T, sin.T], 1), np.concatenate([-sin.T, cos.T], 1)], 0
    )
    high, low = split(along_z)
    z_out = np.zeros((2 * LANES, 2 * n.cells), ml_dtypes.bfloat16)
    z_out[: 2 * n.kf] = high
    z_out[2 * n.kf : 4 * n.kf] = high
    z_out[LANES : LANES + 2 * n.kf] = low
    high, low = split(np.concatenate([cos, -sin], 1))
    y_out = np.concatenate([high, high, low], 1)
    place = np.arange(n.gx)
    freq_rows = np.zeros((n.rows,), np.int64)
    used = np.zeros((n.rows,), np.float64)
    for block in range(n.ta):
        for i in range(n.ib):
            freq_rows[4 * block + i] = freq[block * n.ib + i]
            used[4 * block + i] = 1.0
    angle = 2 * np.pi * ((freq_rows[:, None] * place[None, :]) % n.gx) / n.gx
    x_in = two_terms(np.concatenate([np.cos(angle), -np.sin(angle)], 1) * used[:, None])
    angle = angle.T
    x_out = two_terms(np.concatenate([np.cos(angle) * used, np.sin(angle) * used], 1))
    places, parts, begin = {}, [], 0
    for name, part in (
        ("grid_in", grid_in),
        ("z_out", z_out),
        ("y_out", y_out),
        ("x_in", x_in),
        ("x_out", x_out),
    ):
        rows = -(-part.shape[0] // 16) * 16
        padded = np.zeros((rows, 256), ml_dtypes.bfloat16)
        padded[: part.shape[0], : part.shape[1]] = part
        places[name] = (slice(begin, begin + part.shape[0]), slice(0, part.shape[1]))
        parts.append(padded)
        begin += rows
    return np.concatenate(parts, 0), places


def halves(value):
    high = value.astype(BF16).astype(F32)
    return high, value - high


def dot(left, right):
    return jnp.dot(left, right, preferred_element_type=F32)


def roll(value, amount):
    amount = amount % LANES
    return value if amount == 0 else pltpu.roll(value, amount, 1)


def times_i(value, chans):
    lane = lax.broadcasted_iota(jnp.int32, value.shape, 1)
    return jnp.where(lane % (2 * chans) < chans, -roll(value, -chans), roll(value, chans))


def far_first(step, count):
    return count // 2 + (1 - 2 * (step % 2)) * ((step + 1) // 2)


def synthesis(n, y_out, z_real, z_imag, first):
    sides = []
    for d in (first, first + 1):
        rows = pl.ds(d, n.kf, stride=STRIDE)
        sides.append(jnp.concatenate([z_real[rows, :], z_imag[rows, :]], 0))
    high, low = halves(jnp.concatenate(sides, 1))
    return dot(y_out[...], jnp.concatenate([high, low, high], 0).astype(BF16))


def side_by_side(ref, first):
    return jnp.concatenate([ref[first], ref[first + 1]], 1)


def kernel(
    n,
    factor,
    places,
    field_hbm,
    cotangent_hbm,
    weight_hbm,
    local_hbm,
    tables_hbm,
    layer_out,
    mixed_local,
    z_real,
    z_imag,
    grad_out,
    field,
    cotangent,
    weight_in,
    local,
    tables,
    weight,
    upstream,
    y_cos,
    y_sin,
    pairs,
    stacked,
    turned,
    spec,
    spec_rows,
    grad_rows,
    sent_x,
    got_x,
    sent_t,
    got_t,
    load_sem,
    own_sem,
    send_sem,
    recv_sem,
):
    chans, kf, cells = n.chans, n.kf, n.cells
    gx, ta = lax.axis_index("gx"), lax.axis_index("ta")
    my_y, my_x, my_core = gx // (2 * n.nx), (gx // 2) % n.nx, gx % 2
    mesh_ids = pl.DeviceIdType.MESH
    grid_in, z_out, y_out, x_in, x_out = (
        tables.at[places[name]] for name in ("grid_in", "z_out", "y_out", "x_in", "x_out")
    )

    def x_peer(step):
        y = lax.rem(my_y + far_first(step // (2 * n.nx), n.ny), n.ny)
        x = lax.rem(my_x + far_first((step // 2) % n.nx, n.nx), n.nx)
        core = lax.rem(my_core + 1 - step % 2, 2)
        return (y * n.nx + x) * 2 + core

    def t_peer(step):
        return lax.rem(ta + far_first(step, n.ta), n.ta)

    barrier = pltpu.get_barrier_semaphore()

    def greet_x(step, carry):
        pl.semaphore_signal(
            barrier, inc=1, device_id={"gx": x_peer(step), "ta": ta}, device_id_type=mesh_ids
        )
        return carry

    for step in range(n.ta - 1):
        pl.semaphore_signal(
            barrier, inc=1, device_id={"gx": gx, "ta": t_peer(step)}, device_id_type=mesh_ids
        )
    loads = [
        pltpu.make_async_copy(source, target, load_sem.at[at])
        for at, (source, target) in enumerate(
            (
                (tables_hbm, tables),
                (field_hbm, field),
                (local_hbm, local),
                (weight_hbm, weight_in),
                (cotangent_hbm, cotangent),
            )
        )
    ]
    for load in loads:
        load.start()
    lax.fori_loop(0, n.gx - 1, greet_x, 0)

    def received(block, index):
        return pltpu.make_async_remote_copy(
            src_ref=block,
            dst_ref=block,
            send_sem=send_sem.at[index],
            recv_sem=recv_sem.at[index],
            device_id={"gx": gx, "ta": ta},
            device_id_type=mesh_ids,
        )

    def all_x(index):
        return received(got_x.at[index // 2, pl.ds(0, (n.gx - 1) * n.tiles), :], index)

    def all_t(index):
        return received(got_t.at[index // 2, :, pl.ds(0, (n.ta - 1) * 4), :], index)

    def of_x(ref, index, device):
        return ref.at[index // 2, pl.ds(pl.multiple_of(4 * device, 4), n.tiles), :]

    def of_t(ref, index, device):
        return ref.at[index // 2, :, pl.ds(pl.multiple_of(4 * device, 4), 4), :]

    def exchange_x(index):
        def send(step, carry):
            peer = x_peer(step)
            pltpu.make_async_remote_copy(
                src_ref=of_x(sent_x, index, peer),
                dst_ref=of_x(got_x, index, gx),
                send_sem=send_sem.at[index],
                recv_sem=recv_sem.at[index],
                device_id={"gx": peer, "ta": ta},
                device_id_type=mesh_ids,
            ).start()
            return carry

        lax.fori_loop(0, n.gx - 1, send, 0, unroll=7 if (n.gx - 1) % 7 == 0 else 1)
        pltpu.make_async_copy(
            of_x(sent_x, index, gx), of_x(got_x, index, gx), own_sem.at[index]
        ).start()

    def exchange_t(index):
        for step in range(n.ta - 1):
            peer = t_peer(step)
            pltpu.make_async_remote_copy(
                src_ref=of_t(sent_t, index, peer),
                dst_ref=of_t(got_t, index, ta),
                send_sem=send_sem.at[index],
                recv_sem=recv_sem.at[index],
                device_id={"gx": gx, "ta": peer},
                device_id_type=mesh_ids,
            ).start()
        pltpu.make_async_copy(
            of_t(sent_t, index, ta), of_t(got_t, index, ta), own_sem.at[index]
        ).start()

    def arrived_x(index):
        pltpu.make_async_copy(
            of_x(sent_x, index, gx), of_x(got_x, index, gx), own_sem.at[index]
        ).wait()
        all_x(index).wait_recv()

    def arrived_t(index):
        pltpu.make_async_copy(
            of_t(sent_t, index, ta), of_t(got_t, index, ta), own_sem.at[index]
        ).wait()
        all_t(index).wait_recv()

    def mix_local(source, transposed, start, stop):
        def step(at, carry):
            rows = pl.ds(pl.multiple_of(at * 16, 16), 16)
            values = [source[c, rows, :].astype(F32) for c in range(chans)]
            for d in range(chans):
                total = None
                for c in range(chans):
                    scale = local[d, c] if transposed else local[c, d]
                    term = values[c] * scale
                    total = term if total is None else total + term
                mixed_local[d, rows, :] = total
            return carry

        lax.fori_loop(start, stop, step, 0)

    def turn_weights(part):
        def step(c, carry):
            for block in range(n.blocks):
                pairs[KT * block : KT * block + KT, :chans] = weight_in[part * n.blocks + block, c]
            weight[part, c] = pairs[:LANES, :].T[:chans]
            return carry

        pairs[:LANES, :] = jnp.zeros((LANES, LANES), F32)
        lax.fori_loop(0, chans, step, 0)

    def pack(index):
        parts = []
        for source in (y_cos, y_sin):
            high, low = halves(source[...])
            both = jnp.concatenate([high.astype(BF16), low.astype(BF16)], 1)
            out = lax.dot_general(
                grid_in[...], both, (((1,), (1,)), ((), ())), preferred_element_type=F32
            )
            parts.append(out[: 2 * kf] + out[2 * kf :])
        of_cos, of_sin = parts
        real = of_cos[:kf] - of_sin[kf:]
        imag = -(of_sin[:kf] + of_cos[kf:])
        lane = lax.broadcasted_iota(jnp.int32, (kf, LANES), 1)
        for j in range(kf):
            tile = slice((j // n.fper) * LANES, (j // n.fper + 1) * LANES)
            back = (j % n.fper) * STRIDE
            value = jnp.where(
                lane < chans,
                roll(real[:, tile], -back),
                jnp.where(lane < 2 * chans, roll(imag[:, tile], chans - back), 0.0),
            )
            pairs[j * kf : (j + 1) * kf, :] = value
        for q in range(n.tiles):
            total = None
            for r in range(n.per):
                value = roll(pairs[pl.ds(q * n.per + r, n.gx, stride=n.pb), :], r * n.width)
                total = value if total is None else total + value
            sent_x[index // 2, pl.ds(q, n.gx, stride=4), :] = total

    def unpack(index):
        for q in range(n.tiles):
            received_rows = got_x[index // 2, pl.ds(q, n.gx, stride=4), :]
            for r in range(n.per):
                pairs[pl.ds(q * n.per + r, n.gx, stride=n.pb), :] = roll(
                    received_rows, -r * n.width
                )
        lane = lax.broadcasted_iota(jnp.int32, (kf, LANES), 1)
        for tile in range(n.ftiles):
            real = jnp.zeros((kf, LANES), F32)
            imag = jnp.zeros((kf, LANES), F32)
            for part in range(n.fper):
                j = tile * n.fper + part
                if j >= kf:
                    continue
                value = pairs[j * kf : (j + 1) * kf, :]
                begin = part * STRIDE
                here = (lane >= begin) & (lane < begin + chans)
                real = jnp.where(here, roll(value, begin), real)
                imag = jnp.where(here, roll(value, begin - chans), imag)
            high, low = halves(jnp.concatenate([real, imag], 0))
            pad = jnp.zeros((LANES - 4 * kf, LANES), F32)
            rows = jnp.concatenate([high, low, pad], 0).T.astype(BF16)
            out = dot(jnp.concatenate([rows, rows], 1), z_out[...])
            z_real[tile * LANES : (tile + 1) * LANES, :] = out[:, :cells]
            z_imag[tile * LANES : (tile + 1) * LANES, :] = out[:, cells:]

    def put_y(first, out):
        out = out[: 2 * kf] + out[2 * kf :]
        for side in range(2):
            rows = pl.ds(first + side, kf, stride=STRIDE)
            columns = slice(side * cells, (side + 1) * cells)
            y_cos[rows, :] = out[:kf, columns]
            y_sin[rows, :] = out[kf:, columns]

    def along_x(table, value):
        high, low = halves(jnp.concatenate([value, times_i(value, chans)], 0))
        out = dot(table[...], jnp.concatenate([high, low], 0).astype(BF16))
        half = out.shape[0] // 2
        return out[:half] + out[half:]

    def analysis_x(index):
        for q in range(n.tiles):
            value = got_x[index // 2, pl.ds(q, n.gx, stride=4), :]
            sent_t[(index + 1) // 2, q, :, :] = along_x(x_in, value)

    def synthesis_x(index):
        for q in range(n.tiles):
            value = got_t[index // 2, q, :, :]
            sent_x[(index + 1) // 2, pl.ds(q, n.gx, stride=4), :] = along_x(x_out, value)

    upper = lax.broadcasted_iota(jnp.int32, (8, LANES), 0) < 4

    def time_table(kind, m, pair, weight_m):
        first, second = (
            kind(2 * math.pi * ((m * t) % n.ta) / n.ta) * factor * weight_m
            for t in (2 * pair, 2 * pair + 1)
        )
        return first if first == second else jnp.where(upper, first, second)

    def time_in(index):
        for q in range(n.tiles):
            steps = [got_t[index // 2, q, 8 * u : 8 * u + 8, :] for u in range(n.ta // 2)]
            for m in range(KT):
                real = imag = None
                for u in range(n.ta // 2):
                    first = steps[u] * time_table(math.cos, m, u, 1.0)
                    second = steps[u] * time_table(math.sin, m, u, 1.0)
                    real = first if real is None else real + first
                    imag = second if imag is None else imag + second
                value = real - times_i(imag, chans)
                value = value[:4] + value[4:]
                for r in range(n.per):
                    stacked[
                        pl.ds((q * n.per + r) * KT + m, 4, stride=n.pb * KT), :
                    ] = roll(value, -r * n.width)

    def time_out(index):
        stacked[:LANES, :] = turned[...].T
        for q in range(n.tiles):
            values = []
            for m in range(KT):
                total = None
                for r in range(n.per):
                    rows = pl.ds((q * n.per + r) * KT + m, 4, stride=n.pb * KT)
                    value = roll(stacked[rows, :], r * n.width)
                    total = value if total is None else total + value
                total = jnp.concatenate([total, total], 0)
                values.append((total, times_i(total, chans)))
            for u in range(n.ta // 2):
                total = None
                for m in range(KT):
                    scale = 1.0 if m == 0 else 2.0
                    value = values[m][0] * time_table(math.cos, m, u, scale)
                    value += values[m][1] * time_table(math.sin, m, u, scale)
                    total = value if total is None else total + value
                sent_t[index // 2, q, 8 * u : 8 * u + 8, :] = total

    def grad_weights():
        row = lax.broadcasted_iota(jnp.int32, (8, LANES), 0)
        weights = jnp.where(row % KT == 0, 1.0, 2.0)
        for at in range(0, n.modes, 8):
            rows = slice(at, at + 8)
            ours = spec_rows[rows, :] * weights
            real = grad_rows[rows, :]
            imag = roll(real, -chans)
            real, imag = real[:, :chans], imag[:, :chans]
            for c in range(chans):
                spec_r = jnp.broadcast_to(ours[:, c : c + 1], (8, chans))
                spec_i = jnp.broadcast_to(ours[:, chans + c : chans + c + 1], (8, chans))
                out_r = spec_r * real + spec_i * imag
                out_i = spec_r * imag - spec_i * real
                for part in range(2):
                    block = at // KT + part
                    if block < n.blocks:
                        cut = slice(KT * part, KT * part + KT)
                        grad_out[block, c] = out_r[cut]
                        grad_out[n.blocks + block, c] = out_i[cut]

    def analyse_field(pair, carry):
        put_y(2 * pair, dot(grid_in[:, :cells], side_by_side(field, 2 * pair)))
        return carry

    loads[0].wait()
    loads[1].wait()
    lax.fori_loop(0, chans // 2, analyse_field, 0, unroll=2)
    pack(0)
    pl.semaphore_wait(barrier, n.gx - 1 + n.ta - 1)
    exchange_x(0)
    stacked[...] = jnp.zeros_like(stacked)
    turned[...] = jnp.zeros_like(turned)
    loads[3].wait()
    turn_weights(0)
    turn_weights(1)
    loads[2].wait()
    arrived_x(0)
    analysis_x(0)
    exchange_t(1)
    chunks = cells // 16
    mix_local(field, False, 0, 3 * chunks // 8)
    arrived_t(1)
    time_in(1)
    spec[...] = stacked[:LANES, :].T[: n.width]
    real = jnp.zeros((chans, LANES), F32)
    imag = jnp.zeros((chans, LANES), F32)
    for c in range(chans):
        spec_r, spec_i = spec[c : c + 1, :], spec[chans + c : chans + c + 1, :]
        real += spec_r * weight[0, c] - spec_i * weight[1, c]
        imag += spec_r * weight[1, c] + spec_i * weight[0, c]
    turned[:chans, :] = real
    turned[chans : 2 * chans, :] = imag
    spec_rows[...] = stacked[:LANES, :]
    time_out(2)
    exchange_t(2)
    mix_local(field, False, 3 * chunks // 8, 5 * chunks // 8)
    arrived_t(2)
    synthesis_x(2)
    exchange_x(3)
    mix_local(field, False, 5 * chunks // 8, chunks)
    loads[4].wait()
    arrived_x(3)
    unpack(3)

    def activate(pair, carry):
        first = 2 * pair
        pre_act = side_by_side(mixed_local, first) + synthesis(n, y_out, z_real, z_imag, first)
        normal_cdf = 0.5 * (1.0 + lax.erf(pre_act * (1.0 / math.sqrt(2.0))))
        density = jnp.exp(-0.5 * pre_act * pre_act) * (1.0 / math.sqrt(2.0 * math.pi))
        out = pre_act * normal_cdf
        value = side_by_side(cotangent, first).astype(F32) * (normal_cdf + pre_act * density)
        for side in range(2):
            columns = slice(side * cells, (side + 1) * cells)
            layer_out[first + side] = out[:, columns]
            upstream[first + side] = value[:, columns]
        high, low = halves(value)
        put_y(first, dot(grid_in[...], jnp.concatenate([high, low], 0).astype(BF16)))
        return carry

    lax.fori_loop(0, chans // 2, activate, 0, unroll=2)
    pack(4)
    exchange_x(4)
    mix_local(upstream, True, 0, chunks // 2)
    arrived_x(4)
    analysis_x(4)
    exchange_t(5)
    mix_local(upstream, True, chunks // 2, 3 * chunks // 4)
    arrived_t(5)
    time_in(5)
    grad_rows[...] = stacked[:LANES, :]
    spec[...] = stacked[:LANES, :].T[: n.width]
    grad_r, grad_i = spec[:chans, :], spec[chans : 2 * chans, :]
    for c in range(chans):
        turned[c : c + 1, :] = jnp.sum(
            weight[0, c] * grad_r + weight[1, c] * grad_i, 0, keepdims=True
        )
        turned[chans + c : chans + c + 1, :] = jnp.sum(
            weight[0, c] * grad_i - weight[1, c] * grad_r, 0, keepdims=True
        )
    time_out(6)
    exchange_t(6)
    mix_local(upstream, True, 3 * chunks // 4, chunks)
    arrived_t(6)
    synthesis_x(6)
    exchange_x(7)
    grad_weights()
    arrived_x(7)
    unpack(7)
    for index in range(8):
        (all_x if index in (0, 3, 4, 7) else all_t)(index).wait_send()


def finish(
    n,
    layer_in,
    mixed_local,
    z_real,
    z_imag,
    grad_in,
    y_out,
    layer_out,
    grad_field,
    grad_spectral,
    planes,
    sems,
):
    layer_copy = pltpu.make_async_copy(layer_in, layer_out, sems.at[0])
    layer_copy.start()
    grad_copy = pltpu.make_async_copy(grad_in, grad_spectral, sems.at[1])
    grad_copy.start()

    def step(pair, carry):
        first = 2 * pair
        value = side_by_side(mixed_local, first) + synthesis(n, y_out, z_real, z_imag, first)
        for side in range(2):
            planes[first + side] = value[:, side * n.cells : (side + 1) * n.cells]
        two = pl.ds(first, 2)
        pltpu.make_async_copy(planes.at[two], grad_field.at[two], sems.at[2]).start()
        return carry

    lax.fori_loop(0, n.chans // 2, step, 0, unroll=2)
    layer_copy.wait()
    grad_copy.wait()
    pltpu.make_async_copy(planes, grad_field, sems.at[2]).wait()


def shards(n, factor, field, spectral_weight, local_weight, cotangent):
    chans, cells = n.chans, n.cells
    tables, places = make_tables(n)
    weight = jnp.transpose(spectral_weight, (0, 1, 2, 4, 3, 5))
    weight = weight.reshape(2 * n.blocks, chans, KT, chans)
    vmem = pl.BlockSpec(memory_space=pltpu.VMEM)
    hbm = pl.BlockSpec(memory_space=pltpu.HBM)
    wide = jax.ShapeDtypeStruct((chans, cells, cells), F32)
    halfway = jax.ShapeDtypeStruct((n.frows, cells), F32)
    weights = jax.ShapeDtypeStruct(weight.shape, F32)
    rows = max(n.kf * n.kf, LANES)
    results = pl.pallas_call(
        functools.partial(kernel, n, factor, places),
        out_shape=(wide, wide, halfway, halfway, weights),
        in_specs=[hbm] * 5,
        out_specs=(vmem,) * 5,
        scratch_shapes=[
            pltpu.VMEM((chans, cells, cells), BF16),
            pltpu.VMEM((chans, cells, cells), BF16),
            pltpu.VMEM(weight.shape, F32),
            pltpu.SMEM((chans, chans), F32),
            pltpu.VMEM(tables.shape, BF16),
            pltpu.VMEM((2, chans, chans, LANES), F32),
            pltpu.VMEM((chans, cells, cells), F32),
            pltpu.VMEM((n.frows, cells), F32),
            pltpu.VMEM((n.frows, cells), F32),
            pltpu.VMEM((rows, LANES), F32),
            pltpu.VMEM((4 * n.pb * KT, LANES), F32),
            pltpu.VMEM((LANES, LANES), F32),
            pltpu.VMEM((n.width, LANES), F32),
            pltpu.VMEM((LANES, LANES), F32),
            pltpu.VMEM((LANES, LANES), F32),
            pltpu.VMEM((4, 4 * n.gx, LANES), F32),
            pltpu.VMEM((4, 4 * n.gx, LANES), F32),
            pltpu.VMEM((4, n.tiles, n.rows, LANES), F32),
            pltpu.VMEM((4, n.tiles, n.rows, LANES), F32),
            pltpu.SemaphoreType.DMA((5,)),
            pltpu.SemaphoreType.DMA((8,)),
            pltpu.SemaphoreType.DMA((8,)),
            pltpu.SemaphoreType.DMA((8,)),
        ],
        compiler_params=pltpu.CompilerParams(
            collective_id=0, has_side_effects=True, vmem_limit_bytes=40 * 1024 * 1024
        ),
    )(
        *(
            pltpu.with_memory_space_constraint(value, pltpu.HBM)
            for value in (
                field.reshape(chans, cells, cells),
                cotangent.reshape(chans, cells, cells),
                weight,
                local_weight,
                jnp.asarray(tables),
            )
        )
    )
    layer_out, grad_field, grad_spectral = pl.pallas_call(
        functools.partial(finish, n),
        out_shape=(wide, wide, weights),
        in_specs=[vmem] * 6,
        out_specs=(hbm,) * 3,
        scratch_shapes=[
            pltpu.VMEM((chans, cells, cells), F32),
            pltpu.SemaphoreType.DMA((3,)),
        ],
        compiler_params=pltpu.CompilerParams(vmem_limit_bytes=16 * 1024 * 1024),
    )(*results, jnp.asarray(tables[places["y_out"]]))
    grad_spectral = grad_spectral.reshape(2, n.ib, n.pb, chans, KT, chans)
    grad_spectral = jnp.transpose(grad_spectral, (0, 1, 2, 4, 3, 5))
    return (layer_out.reshape(field.shape), grad_field.reshape(field.shape), grad_spectral)


def solution(mesh, chans=20, kf=24, cells=128):
    n = Sizes(mesh.shape["gx"], mesh.shape["ta"], chans, kf, cells)
    factor = 1.0 / math.sqrt(n.gx * n.ta * cells * cells)
    grid = P(None, "ta", "gx", None, None)
    modes = P(None, "ta", "gx", None, None, None)
    return jax.shard_map(
        functools.partial(shards, n, factor),
        mesh=mesh,
        in_specs=(grid, modes, P(), grid),
        out_specs=(grid, grid, modes),
        check_vma=False,
    )
```

time: 104 us -> 70.4 us (0.68)
  Pallas kernels: 88.3 us -> 69.6 us
  local copies, waits for them, and re-layouts: 11 us -> 0.01 us
  other arithmetic: 3.41 us -> 0 us
    pallas_call x1 -> x2, Pallas kernels: 88.3 us -> 69.6 us  [the longest x1 67.3 us: shards(): pl.pallas_call(functools.partial(kernel, n, factor, places), out_shape=(w...]
    unnamed x19 -> x2, local copies, waits for them, and re-layouts: 6.61 us -> 0.01 us
    reshape x1 -> x0, local copies, waits for them, and re-layouts: 2.17 us -> none  [shards(): weight = spectral_weight.reshape(2, n.modes, chans, chans)]
    another operation x1 -> x0, other arithmetic: 1.93 us -> none  [shards(): jnp.stack([spec_r * grad_r + spec_i * grad_i, spec_r * grad_i - spec_i *...]
    add x1 -> x0, other arithmetic: 1.39 us -> none  [shards(): spec_r * grad_r + spec_i * grad_i]
    pad x1 -> x0, local copies, waits for them, and re-layouts: 1.13 us -> none  [shards(): weight = jnp.pad(weight, ((0, 0), (0, 0), (0, 0), (0, LANES - n.modes)))]
where the time goes in v2:
time: 70.4 us; the launch traced here: 70.2 us
  Pallas kernels  69.6 us (99%)
    pallas_call x1, Pallas kernels, shards(): pl.pallas_call(functools.partial(kernel, n, factor, places), out_shape=(w...  67.3 us
    pallas_call x1, Pallas kernels, shards(): pl.pallas_call(functools.partial(finish, n), out_shape=(wide, wide, weigh...  2.22 us

profile of v2, /device:TPU:1, one launch (start us, length us, event | category | flops | bytes accessed | tf_op | source)
XLA Modules:
  0.0 70.2 jit_solution(2691335570456560955)
XLA Ops:
  0.6 0.0 copy-start
  0.6 67.3 %shard_map.85 = (f32[20,128,128]{2,1,0:T(8,128)S(1)}, f32[20,128,128]{2,1,0:T(8,128)S(1)}, f32[768,128]{1,0:T(8,128)S(1)}, f32[768,128]{1,0:T(8,128)S(1)}, f32[54,20,4,20]{3,2,1,0:T(4,128)S(1)}) custom-call(bf16[20,128,128]{2,1,0:T(8,128)(2,1)} %bitcast.15, bf16[20,128,128]{2,1,0:T(8,128)(2,1)} %bitcast.16, f32[54,20,4,20]{3,2,1,0:T(4,128)} %bitcast.14, ...), custom_call_target="tpu_custom_call" | custom-call | tf_op jit(solution)/shard_map/pallas_call | solution.py:592
  68.0 0.0 copy-done
  68.0 2.2 %shard_map.86 = (f32[20,128,128]{2,1,0:T(8,128)}, f32[20,128,128]{2,1,0:T(8,128)}, f32[54,20,4,20]{3,2,1,0:T(4,128)}) custom-call(f32[20,128,128]{2,1,0:T(8,128)S(1)} %get-tuple-element.11.layer_in, f32[20,128,128]{2,1,0:T(8,128)S(1)} %get-tuple-element.12.mixed_local, f32[768,128]{1,0:T(8,128)S(1)} %get-tuple-element.13.z_real, ...), custom_call_target="tpu_custom_call" | custom-call | tf_op jit(solution)/shard_map/pallas_call | solution.py:637
Async XLA Ops:
  0.6 67.4 %copy-start = (bf16[128,144]{1,0:T(8,128)(2,1)S(1)}, bf16[128,144]{1,0:T(8,128)(2,1)}, u32[]{:S(2)}) copy-start(bf16[128,144]{1,0:T(8,128)(2,1)} %constant.5.clone.y_out) | copy-start | bytes 110596

commit v3 on v2

--- a/solution.py
+++ b/solution.py
@@ -13,6 +13,7 @@
 KT = 4
 STRIDE = 32
 LANES = 128
+PIECES = 4
 F32 = jnp.float32
 BF16 = jnp.bfloat16
 
@@ -169,29 +170,39 @@
 ):
     chans, kf, cells = n.chans, n.kf, n.cells
     gx, ta = lax.axis_index("gx"), lax.axis_index("ta")
-    my_y, my_x, my_core = gx // (2 * n.nx), (gx // 2) % n.nx, gx % 2
+    my_y, my_x, my_core = lax.div(gx, 2 * n.nx), lax.rem(lax.div(gx, 2), n.nx), lax.rem(gx, 2)
     mesh_ids = pl.DeviceIdType.MESH
     grid_in, z_out, y_out, x_in, x_out = (
         tables.at[places[name]] for name in ("grid_in", "z_out", "y_out", "x_in", "x_out")
     )
 
-    def x_peer(step):
-        y = lax.rem(my_y + far_first(step // (2 * n.nx), n.ny), n.ny)
-        x = lax.rem(my_x + far_first((step // 2) % n.nx, n.nx), n.nx)
-        core = lax.rem(my_core + 1 - step % 2, 2)
-        return (y * n.nx + x) * 2 + core
+    places_xc = []
+    for step in range(2 * n.nx):
+        x = lax.rem(my_x + far_first(step // 2, n.nx), n.nx)
+        places_xc.append(2 * x + lax.rem(my_core + 1 - step % 2, 2))
+
+    def each_x_peer(act):
+        def row(step, carry):
+            y = lax.rem(my_y + far_first(step, n.ny), n.ny) * (2 * n.nx)
+            for place in places_xc:
+                act(y + place)
+            return carry
+
+        lax.fori_loop(0, n.ny - 1, row, 0)
+        for place in places_xc[:-1]:
+            act(my_y * (2 * n.nx) + place)
 
     def t_peer(step):
         return lax.rem(ta + far_first(step, n.ta), n.ta)
 
     barrier = pltpu.get_barrier_semaphore()
 
-    def greet_x(step, carry):
+    def greet_x(device):
         pl.semaphore_signal(
-            barrier, inc=1, device_id={"gx": x_peer(step), "ta": ta}, device_id_type=mesh_ids
-        )
-        return carry
-
+            barrier, inc=1, device_id={"gx": device, "ta": ta}, device_id_type=mesh_ids
+        )
+
+    each_x_peer(greet_x)
     for step in range(n.ta - 1):
         pl.semaphore_signal(
             barrier, inc=1, device_id={"gx": gx, "ta": t_peer(step)}, device_id_type=mesh_ids
@@ -208,9 +219,8 @@
             )
         )
     ]
-    for load in loads:
-        load.start()
-    lax.fori_loop(0, n.gx - 1, greet_x, 0)
+    loads[0].start()
+    loads[1].start()
 
     def received(block, index):
         return pltpu.make_async_remote_copy(
@@ -235,8 +245,7 @@
         return ref.at[index // 2, :, pl.ds(pl.multiple_of(4 * device, 4), 4), :]
 
     def exchange_x(index):
-        def send(step, carry):
-            peer = x_peer(step)
+        def send(peer):
             pltpu.make_async_remote_copy(
                 src_ref=of_x(sent_x, index, peer),
                 dst_ref=of_x(got_x, index, gx),
@@ -245,9 +254,8 @@
                 device_id={"gx": peer, "ta": ta},
                 device_id_type=mesh_ids,
             ).start()
-            return carry
-
-        lax.fori_loop(0, n.gx - 1, send, 0, unroll=7 if (n.gx - 1) % 7 == 0 else 1)
+
+        each_x_peer(send)
         pltpu.make_async_copy(
             of_x(sent_x, index, gx), of_x(got_x, index, gx), own_sem.at[index]
         ).start()
@@ -341,6 +349,7 @@
                     received_rows, -r * n.width
                 )
         lane = lax.broadcasted_iota(jnp.int32, (kf, LANES), 1)
+        all_rows = []
         for tile in range(n.ftiles):
             real = jnp.zeros((kf, LANES), F32)
             imag = jnp.zeros((kf, LANES), F32)
@@ -355,10 +364,11 @@
                 imag = jnp.where(here, roll(value, begin - chans), imag)
             high, low = halves(jnp.concatenate([real, imag], 0))
             pad = jnp.zeros((LANES - 4 * kf, LANES), F32)
-            rows = jnp.concatenate([high, low, pad], 0).T.astype(BF16)
-            out = dot(jnp.concatenate([rows, rows], 1), z_out[...])
-            z_real[tile * LANES : (tile + 1) * LANES, :] = out[:, :cells]
-            z_imag[tile * LANES : (tile + 1) * LANES, :] = out[:, cells:]
+            all_rows.append(jnp.concatenate([high, low, pad], 0).T.astype(BF16))
+        rows = jnp.concatenate(all_rows, 0)
+        out = dot(jnp.concatenate([rows, rows], 1), z_out[...])
+        z_real[...] = out[:, :cells]
+        z_imag[...] = out[:, cells:]
 
     def put_y(first, out):
         out = out[: 2 * kf] + out[2 * kf :]
@@ -368,21 +378,23 @@
             y_cos[rows, :] = out[:kf, columns]
             y_sin[rows, :] = out[kf:, columns]
 
-    def along_x(table, value):
-        high, low = halves(jnp.concatenate([value, times_i(value, chans)], 0))
-        out = dot(table[...], jnp.concatenate([high, low], 0).astype(BF16))
+    def along_x(table, values):
+        pairs_of = [halves(jnp.concatenate([v, times_i(v, chans)], 0)) for v in values]
+        both = [jnp.concatenate([high, low], 0).astype(BF16) for high, low in pairs_of]
+        out = dot(table[...], jnp.concatenate(both, 1))
         half = out.shape[0] // 2
-        return out[:half] + out[half:]
+        out = out[:half] + out[half:]
+        return [out[:, q * LANES : (q + 1) * LANES] for q in range(n.tiles)]
 
     def analysis_x(index):
-        for q in range(n.tiles):
-            value = got_x[index // 2, pl.ds(q, n.gx, stride=4), :]
-            sent_t[(index + 1) // 2, q, :, :] = along_x(x_in, value)
+        values = [got_x[index // 2, pl.ds(q, n.gx, stride=4), :] for q in range(n.tiles)]
+        for q, value in enumerate(along_x(x_in, values)):
+            sent_t[(index + 1) // 2, q, :, :] = value
 
     def synthesis_x(index):
-        for q in range(n.tiles):
-            value = got_t[index // 2, q, :, :]
-            sent_x[(index + 1) // 2, pl.ds(q, n.gx, stride=4), :] = along_x(x_out, value)
+        values = [got_t[index // 2, q, :, :] for q in range(n.tiles)]
+        for q, value in enumerate(along_x(x_out, values)):
+            sent_x[(index + 1) // 2, pl.ds(q, n.gx, stride=4), :] = value
 
     upper = lax.broadcasted_iota(jnp.int32, (8, LANES), 0) < 4
 
@@ -458,7 +470,9 @@
 
     loads[0].wait()
     loads[1].wait()
-    lax.fori_loop(0, chans // 2, analyse_field, 0, unroll=2)
+    for load in loads[2:]:
+        load.start()
+    lax.fori_loop(0, chans // 2, analyse_field, 0, unroll=5)
     pack(0)
     pl.semaphore_wait(barrier, n.gx - 1 + n.ta - 1)
     exchange_x(0)
@@ -511,7 +525,7 @@
         put_y(first, dot(grid_in[...], jnp.concatenate([high, low], 0).astype(BF16)))
         return carry
 
-    lax.fori_loop(0, chans // 2, activate, 0, unroll=2)
+    lax.fori_loop(0, chans // 2, activate, 0, unroll=5)
     pack(4)
     exchange_x(4)
     mix_local(upstream, True, 0, chunks // 2)
@@ -558,10 +572,18 @@
     planes,
     sems,
 ):
-    layer_copy = pltpu.make_async_copy(layer_in, layer_out, sems.at[0])
-    layer_copy.start()
-    grad_copy = pltpu.make_async_copy(grad_in, grad_spectral, sems.at[1])
-    grad_copy.start()
+    pieces = []
+    for source, target in ((grad_in, grad_spectral), (layer_in, layer_out)):
+        count = source.shape[0] // PIECES
+        for piece in range(PIECES):
+            begin = piece * count
+            end = begin + count if piece < PIECES - 1 else source.shape[0]
+            part = pl.ds(begin, end - begin)
+            pieces.append(
+                pltpu.make_async_copy(source.at[part], target.at[part], sems.at[1 + len(pieces)])
+            )
+    for copy in pieces:
+        copy.start()
 
     def step(pair, carry):
         first = 2 * pair
@@ -569,13 +591,13 @@
         for side in range(2):
             planes[first + side] = value[:, side * n.cells : (side + 1) * n.cells]
         two = pl.ds(first, 2)
-        pltpu.make_async_copy(planes.at[two], grad_field.at[two], sems.at[2]).start()
+        pltpu.make_async_copy(planes.at[two], grad_field.at[two], sems.at[0]).start()
         return carry
 
-    lax.fori_loop(0, n.chans // 2, step, 0, unroll=2)
-    layer_copy.wait()
-    grad_copy.wait()
-    pltpu.make_async_copy(planes, grad_field, sems.at[2]).wait()
+    lax.fori_loop(0, n.chans // 2, step, 0, unroll=5)
+    for copy in pieces:
+        copy.wait()
+    pltpu.make_async_copy(planes, grad_field, sems.at[0]).wait()
 
 
 def shards(n, factor, field, spectral_weight, local_weight, cotangent):
@@ -641,7 +663,7 @@
         out_specs=(hbm,) * 3,
         scratch_shapes=[
             pltpu.VMEM((chans, cells, cells), F32),
-            pltpu.SemaphoreType.DMA((3,)),
+            pltpu.SemaphoreType.DMA((1 + 2 * PIECES,)),
         ],
         compiler_params=pltpu.CompilerParams(vmem_limit_bytes=16 * 1024 * 1024),
     )(*results, jnp.asarray(tables[places["y_out"]]))

time: 70.4 us -> 67.4 us (0.957)
  Pallas kernels: 69.6 us -> 66.5 us
    pallas_call x1, Pallas kernels: 67.3 us -> 64.3 us  [shards(): pl.pallas_call(functools.partial(kernel, n, factor, places), out_shape=(w...]
where the time goes in v3:
time: 67.4 us; the launch traced here: 67.2 us
  Pallas kernels  66.5 us (99%)
    pallas_call x1, Pallas kernels, shards(): pl.pallas_call(functools.partial(kernel, n, factor, places), out_shape=(w...  64.3 us
    pallas_call x1, Pallas kernels, shards(): pl.pallas_call(functools.partial(finish, n), out_shape=(wide, wide, weigh...  2.27 us

profile of v3, /device:TPU:1, one launch (start us, length us, event | category | flops | bytes accessed | tf_op | source)
XLA Modules:
  0.0 67.2 jit_solution(10007649598675305546)
XLA Ops:
  0.6 0.0 copy-start
  0.6 64.3 %shard_map.85 = (f32[20,128,128]{2,1,0:T(8,128)S(1)}, f32[20,128,128]{2,1,0:T(8,128)S(1)}, f32[768,128]{1,0:T(8,128)S(1)}, f32[768,128]{1,0:T(8,128)S(1)}, f32[54,20,4,20]{3,2,1,0:T(4,128)S(1)}) custom-call(bf16[20,128,128]{2,1,0:T(8,128)(2,1)} %bitcast.15, bf16[20,128,128]{2,1,0:T(8,128)(2,1)} %bitcast.16, f32[54,20,4,20]{3,2,1,0:T(4,128)} %bitcast.14, ...), custom_call_target="tpu_custom_call" | custom-call | tf_op jit(solution)/shard_map/pallas_call | solution.py:614
  64.9 0.0 copy-done
  64.9 2.3 %shard_map.86 = (f32[20,128,128]{2,1,0:T(8,128)}, f32[20,128,128]{2,1,0:T(8,128)}, f32[54,20,4,20]{3,2,1,0:T(4,128)}) custom-call(f32[20,128,128]{2,1,0:T(8,128)S(1)} %get-tuple-element.11.layer_in, f32[20,128,128]{2,1,0:T(8,128)S(1)} %get-tuple-element.12.mixed_local, f32[768,128]{1,0:T(8,128)S(1)} %get-tuple-element.13.z_real, ...), custom_call_target="tpu_custom_call" | custom-call | tf_op jit(solution)/shard_map/pallas_call | solution.py:659
Async XLA Ops:
  0.6 64.3 %copy-start = (bf16[128,144]{1,0:T(8,128)(2,1)S(1)}, bf16[128,144]{1,0:T(8,128)(2,1)}, u32[]{:S(2)}) copy-start(bf16[128,144]{1,0:T(8,128)(2,1)} %constant.5.clone.y_out) | copy-start | bytes 110596

commit v4 on v3

--- a/solution.py
+++ b/solution.py
@@ -13,7 +13,6 @@
 KT = 4
 STRIDE = 32
 LANES = 128
-PIECES = 4
 F32 = jnp.float32
 BF16 = jnp.bfloat16
 
@@ -214,7 +213,7 @@
                 (tables_hbm, tables),
                 (field_hbm, field),
                 (local_hbm, local),
-                (weight_hbm, weight_in),
+                (weight_hbm, weight_in.at[pl.ds(0, 2 * n.blocks)]),
                 (cotangent_hbm, cotangent),
             )
         )
@@ -489,7 +488,7 @@
     mix_local(field, False, 0, 3 * chunks // 8)
     arrived_t(1)
     time_in(1)
-    spec[...] = stacked[:LANES, :].T[: n.width]
+    spec[...] = stacked[:LANES, :].T
     real = jnp.zeros((chans, LANES), F32)
     imag = jnp.zeros((chans, LANES), F32)
     for c in range(chans):
@@ -536,7 +535,7 @@
     arrived_t(5)
     time_in(5)
     grad_rows[...] = stacked[:LANES, :]
-    spec[...] = stacked[:LANES, :].T[: n.width]
+    spec[...] = stacked[:LANES, :].T
     grad_r, grad_i = spec[:chans, :], spec[chans : 2 * chans, :]
     for c in range(chans):
         turned[c : c + 1, :] = jnp.sum(
@@ -572,16 +571,12 @@
     planes,
     sems,
 ):
-    pieces = []
-    for source, target in ((grad_in, grad_spectral), (layer_in, layer_out)):
-        count = source.shape[0] // PIECES
-        for piece in range(PIECES):
-            begin = piece * count
-            end = begin + count if piece < PIECES - 1 else source.shape[0]
-            part = pl.ds(begin, end - begin)
-            pieces.append(
-                pltpu.make_async_copy(source.at[part], target.at[part], sems.at[1 + len(pieces)])
-            )
+    pieces = [
+        pltpu.make_async_copy(
+            grad_in.at[pl.ds(0, grad_spectral.shape[0])], grad_spectral, sems.at[1]
+        ),
+        pltpu.make_async_copy(layer_in, layer_out, sems.at[2]),
+    ]
     for copy in pieces:
         copy.start()
 
@@ -610,16 +605,17 @@
     wide = jax.ShapeDtypeStruct((chans, cells, cells), F32)
     halfway = jax.ShapeDtypeStruct((n.frows, cells), F32)
     weights = jax.ShapeDtypeStruct(weight.shape, F32)
+    roomy = (weight.shape[0] + 1,) + weight.shape[1:]
     rows = max(n.kf * n.kf, LANES)
     results = pl.pallas_call(
         functools.partial(kernel, n, factor, places),
-        out_shape=(wide, wide, halfway, halfway, weights),
+        out_shape=(wide, wide, halfway, halfway, jax.ShapeDtypeStruct(roomy, F32)),
         in_specs=[hbm] * 5,
         out_specs=(vmem,) * 5,
         scratch_shapes=[
             pltpu.VMEM((chans, cells, cells), BF16),
             pltpu.VMEM((chans, cells, cells), BF16),
-            pltpu.VMEM(weight.shape, F32),
+            pltpu.VMEM(roomy, F32),
             pltpu.SMEM((chans, chans), F32),
             pltpu.VMEM(tables.shape, BF16),
             pltpu.VMEM((2, chans, chans, LANES), F32),
@@ -627,9 +623,9 @@
             pltpu.VMEM((n.frows, cells), F32),
             pltpu.VMEM((n.frows, cells), F32),
             pltpu.VMEM((rows, LANES), F32),
-            pltpu.VMEM((4 * n.pb * KT, LANES), F32),
+            pltpu.VMEM((8 * n.pb * KT, LANES), F32),
             pltpu.VMEM((LANES, LANES), F32),
-            pltpu.VMEM((n.width, LANES), F32),
+            pltpu.VMEM((LANES, LANES), F32),
             pltpu.VMEM((LANES, LANES), F32),
             pltpu.VMEM((LANES, LANES), F32),
             pltpu.VMEM((4, 4 * n.gx, LANES), F32),
@@ -663,7 +659,7 @@
         out_specs=(hbm,) * 3,
         scratch_shapes=[
             pltpu.VMEM((chans, cells, cells), F32),
-            pltpu.SemaphoreType.DMA((1 + 2 * PIECES,)),
+            pltpu.SemaphoreType.DMA((3,)),
         ],
         compiler_params=pltpu.CompilerParams(vmem_limit_bytes=16 * 1024 * 1024),
     )(*results, jnp.asarray(tables[places["y_out"]]))

time: 67.4 us -> 67.3 us (level)
  no operation moved by 1% of the time
where the time goes in v4:
time: 67.3 us; the launch traced here: 67.2 us
  Pallas kernels  66.5 us (99%)
    pallas_call x1, Pallas kernels, shards(): pl.pallas_call(functools.partial(kernel, n, factor, places), out_shape=(w...  64.3 us
    pallas_call x1, Pallas kernels, shards(): pl.pallas_call(functools.partial(finish, n), out_shape=(wide, wide, weigh...  2.22 us

profile of v4, /device:TPU:1, one launch (start us, length us, event | category | flops | bytes accessed | tf_op | source)
XLA Modules:
  0.0 67.2 jit_solution(7287446469064780711)
XLA Ops:
  0.6 0.0 copy-start
  0.6 64.3 %shard_map.85 = (f32[20,128,128]{2,1,0:T(8,128)S(1)}, f32[20,128,128]{2,1,0:T(8,128)S(1)}, f32[768,128]{1,0:T(8,128)S(1)}, f32[768,128]{1,0:T(8,128)S(1)}, f32[55,20,4,20]{3,2,1,0:T(4,128)S(1)}) custom-call(bf16[20,128,128]{2,1,0:T(8,128)(2,1)} %bitcast.15, bf16[20,128,128]{2,1,0:T(8,128)(2,1)} %bitcast.16, f32[54,20,4,20]{3,2,1,0:T(4,128)} %bitcast.14, ...), custom_call_target="tpu_custom_call" | custom-call | tf_op jit(solution)/shard_map/pallas_call | solution.py:610
  64.9 0.0 copy-done
  64.9 2.2 %shard_map.86 = (f32[20,128,128]{2,1,0:T(8,128)}, f32[20,128,128]{2,1,0:T(8,128)}, f32[54,20,4,20]{3,2,1,0:T(4,128)}) custom-call(f32[20,128,128]{2,1,0:T(8,128)S(1)} %get-tuple-element.11.layer_in, f32[20,128,128]{2,1,0:T(8,128)S(1)} %get-tuple-element.12.mixed_local, f32[768,128]{1,0:T(8,128)S(1)} %get-tuple-element.13.z_real, ...), custom_call_target="tpu_custom_call" | custom-call | tf_op jit(solution)/shard_map/pallas_call | solution.py:655
Async XLA Ops:
  0.6 64.3 %copy-start = (bf16[128,144]{1,0:T(8,128)(2,1)S(1)}, bf16[128,144]{1,0:T(8,128)(2,1)}, u32[]{:S(2)}) copy-start(bf16[128,144]{1,0:T(8,128)(2,1)} %constant.5.clone.y_out) | copy-start | bytes 110596

commit v5 on v4

--- a/solution.py
+++ b/solution.py
@@ -109,7 +109,10 @@
 
 def times_i(value, chans):
     lane = lax.broadcasted_iota(jnp.int32, value.shape, 1)
-    return jnp.where(lane % (2 * chans) < chans, -roll(value, -chans), roll(value, chans))
+    real = lane < chans
+    for begin in range(2 * chans, LANES, 2 * chans):
+        real = real | ((lane >= begin) & (lane < begin + chans))
+    return jnp.where(real, -roll(value, -chans), roll(value, chans))
 
 
 def far_first(step, count):
@@ -326,13 +329,12 @@
         lane = lax.broadcasted_iota(jnp.int32, (kf, LANES), 1)
         for j in range(kf):
             tile = slice((j // n.fper) * LANES, (j // n.fper + 1) * LANES)
-            back = (j % n.fper) * STRIDE
-            value = jnp.where(
-                lane < chans,
-                roll(real[:, tile], -back),
-                jnp.where(lane < 2 * chans, roll(imag[:, tile], chans - back), 0.0),
-            )
-            pairs[j * kf : (j + 1) * kf, :] = value
+            begin = (j % n.fper) * STRIDE
+            if begin == 0:
+                beside = roll(imag[:, tile], chans)
+            here = (lane >= begin) & (lane < begin + chans)
+            value = roll(jnp.where(here, real[:, tile], beside), -begin)
+            pairs[j * kf : (j + 1) * kf, :] = jnp.where(lane < 2 * chans, value, 0.0)
         for q in range(n.tiles):
             total = None
             for r in range(n.per):
@@ -358,9 +360,16 @@
                     continue
                 value = pairs[j * kf : (j + 1) * kf, :]
                 begin = part * STRIDE
-                here = (lane >= begin) & (lane < begin + chans)
-                real = jnp.where(here, roll(value, begin), real)
-                imag = jnp.where(here, roll(value, begin - chans), imag)
+                value = roll(value, begin)
+                real = jnp.where((lane >= begin) & (lane < begin + chans), value, real)
+                first = (begin + chans) % LANES
+                last = (begin + 2 * chans) % LANES
+                if first < last:
+                    beside = (lane >= first) & (lane < last)
+                else:
+                    beside = (lane >= first) | (lane < last)
+                imag = jnp.where(beside, value, imag)
+            imag = roll(imag, -chans)
             high, low = halves(jnp.concatenate([real, imag], 0))
             pad = jnp.zeros((LANES - 4 * kf, LANES), F32)
             all_rows.append(jnp.concatenate([high, low, pad], 0).T.astype(BF16))

time: 67.3 us -> 67.4 us (level)
  no operation moved by 1% of the time
where the time goes in v5:
time: 67.4 us; the launch traced here: 67.2 us
  Pallas kernels  66.6 us (99%)
    pallas_call x1, Pallas kernels, shards(): pl.pallas_call(functools.partial(kernel, n, factor, places), out_shape=(w...  64.3 us
    pallas_call x1, Pallas kernels, shards(): pl.pallas_call(functools.partial(finish, n), out_shape=(wide, wide, weigh...  2.22 us

profile of v5, /device:TPU:1, one launch (start us, length us, event | category | flops | bytes accessed | tf_op | source)
XLA Modules:
  0.0 67.2 jit_solution(8655204302018439307)
XLA Ops:
  0.6 0.0 copy-start
  0.6 64.3 %shard_map.85 = (f32[20,128,128]{2,1,0:T(8,128)S(1)}, f32[20,128,128]{2,1,0:T(8,128)S(1)}, f32[768,128]{1,0:T(8,128)S(1)}, f32[768,128]{1,0:T(8,128)S(1)}, f32[55,20,4,20]{3,2,1,0:T(4,128)S(1)}) custom-call(bf16[20,128,128]{2,1,0:T(8,128)(2,1)} %bitcast.15, bf16[20,128,128]{2,1,0:T(8,128)(2,1)} %bitcast.16, f32[54,20,4,20]{3,2,1,0:T(4,128)} %bitcast.14, ...), custom_call_target="tpu_custom_call" | custom-call | tf_op jit(solution)/shard_map/pallas_call | solution.py:619
  65.0 0.0 copy-done
  65.0 2.2 %shard_map.86 = (f32[20,128,128]{2,1,0:T(8,128)}, f32[20,128,128]{2,1,0:T(8,128)}, f32[54,20,4,20]{3,2,1,0:T(4,128)}) custom-call(f32[20,128,128]{2,1,0:T(8,128)S(1)} %get-tuple-element.11.layer_in, f32[20,128,128]{2,1,0:T(8,128)S(1)} %get-tuple-element.12.mixed_local, f32[768,128]{1,0:T(8,128)S(1)} %get-tuple-element.13.z_real, ...), custom_call_target="tpu_custom_call" | custom-call | tf_op jit(solution)/shard_map/pallas_call | solution.py:664
Async XLA Ops:
  0.6 64.4 %copy-start = (bf16[128,144]{1,0:T(8,128)(2,1)S(1)}, bf16[128,144]{1,0:T(8,128)(2,1)}, u32[]{:S(2)}) copy-start(bf16[128,144]{1,0:T(8,128)(2,1)} %constant.5.clone.y_out) | copy-start | bytes 110596
